TPU v7x, 32 devices: a whole 2x2x4 slice. The times are simulated.
32 devices in a mesh: section: 2 (over x), dp: 4 (over y, core), tensor: 4 (over z).
Axes of the slice: x: 2, y: 2, z: 4, core: 2. Of those that a mesh axis runs over, the one named last changes fastest.
Arguments:
- inputs: bfloat16 [2, 8, 1024, 512], P('section', 'dp', 'tensor'), may hold values from -6 to 6
- cotangent: bfloat16 [2, 8, 1024, 512], P('section', 'dp', 'tensor'), may hold values from -6 to 6
- lengths: int32 [2, 8, 8], P(None, 'dp'), may hold values from 0 to 1024, as said below
- row_flags: int32 [8], P('dp'), may hold values from 0 to 1, as said below
- qkv_w: bfloat16 [2, 3, 512, 512], P('section', None, None, 'tensor'), may hold values from -0.25 to 0.25
- out_w: bfloat16 [2, 512, 512], P('section', 'tensor'), may hold values from -0.75 to 0.75
- cross_w: bfloat16 [2, 2, 512, 512], P('section', None, None, 'tensor'), may hold values from -0.375 to 0.375
- up_w: bfloat16 [2, 512, 2048], P('section', None, 'tensor'), may hold values from -0.25 to 0.25
- down_w: bfloat16 [2, 2048, 512], P('section', 'tensor'), may hold values from -0.125 to 0.125
- norm_gain: float32 [2, 2, 512], replicated, may hold values from 0.5 to 1.5
- norm_bias: float32 [2, 2, 512], replicated, may hold values from -1.5 to 1.5
- cross_gain: float32 [512], replicated, may hold values from 0.5 to 1.5
- cross_bias: float32 [512], replicated, may hold values from -1.5 to 1.5
Outputs:
- outputs: bfloat16 [2, 8, 1024, 512], P('section', 'dp', 'tensor')
- input_grad: float32 [2, 8, 1024, 512], P('section', 'dp', 'tensor')
- qkv_grad: float32 [2, 3, 512, 512], P('section', None, None, 'tensor')
- out_grad: float32 [2, 512, 512], P('section', 'tensor')
- cross_grad: float32 [2, 2, 512, 512], P('section', None, None, 'tensor')
- up_grad: float32 [2, 512, 2048], P('section', None, 'tensor')
- down_grad: float32 [2, 2048, 512], P('section', 'tensor')
- norm_gain_grad: float32 [2, 2, 512], replicated
- norm_bias_grad: float32 [2, 2, 512], replicated
- cross_gain_grad: float32 [512], replicated
- cross_bias_grad: float32 [512], replicated
Inputs may be any that keep to these rules, and one draw needn't show every extreme that they name: `lengths`: for a row with flag 1, entry 0 of each side is the length of its one pair and later entries are 0; for a row with flag 0, entry j is the length of the pair in slot j of 128 positions, 1 to 128. In each aligned block of 2 rows, one row has flag 1 and length 1024 on both sides. `row_flags`: in each aligned block of 2 rows, one or more rows have flag 1.
All inputs are finite; a program needn't handle non-finite values.
Results may differ from a plain program's by a relative error of at most 0.04.
Values may be sent and summed in bfloat16 or wider, within the bound.
No kernel may reach another device: no remote copies, remote signals or barrier semaphores. Data moves between devices by JAX's collectives and lax.ppermute only.
A program may use at most 192 MiB of HBM per device.

v0:
```python
import jax
import jax.numpy as jnp
from jax import lax
from jax.sharding import PartitionSpec as P

HD = 64
LEN = 1024
SYNTH_SLOT_LEN = 128
MB = 2


NEG = -1e30
EPS = 1e-05


def passed_along(block, axis, distance):
    devices = range(lax.axis_size(axis))
    route = [(i - distance, i) for i in devices if i - distance in devices]
    return lax.ppermute(block, axis, route)


def spread_first(rows_low):
    return lax.all_gather(rows_low, "tensor", axis=1, tiled=True)


def spread_next(rows_low):
    return lax.all_gather(rows_low, "tensor", axis=1, tiled=True)


def collect(partial_value):
    return lax.psum_scatter(
        partial_value.astype(jnp.bfloat16), "tensor", scatter_dimension=1, tiled=True
    ).astype(jnp.float32)


def spread_grad(rows_low):
    return lax.all_gather(rows_low, "tensor", axis=1, tiled=True)


def collect_grad(partial_value):
    return lax.psum_scatter(
        partial_value.astype(jnp.bfloat16), "tensor", scatter_dimension=1, tiled=True
    ).astype(jnp.float32)


def layer_norm(resid, gain, bias_vec):
    mean_removed = resid - jnp.mean(resid, axis=-1, keepdims=True)
    inverse = lax.rsqrt(jnp.mean(mean_removed * mean_removed, axis=-1, keepdims=True) + EPS)
    normed = mean_removed * inverse
    return (normed * gain + bias_vec, normed, inverse)


def norm_back(grad_out, normed, inverse, gain):
    scaled = grad_out * gain
    back = inverse * (
        scaled
        - jnp.mean(scaled, axis=-1, keepdims=True)
        - normed * jnp.mean(scaled * normed, axis=-1, keepdims=True)
    )
    return (back, jnp.sum(grad_out * normed, axis=(0, 1)), jnp.sum(grad_out, axis=(0, 1)))


def row_info(lens, row_flag):
    positions = jnp.arange(LEN, dtype=jnp.int32)
    slot_size = jnp.where(row_flag[:, None] == 1, LEN, SYNTH_SLOT_LEN).astype(jnp.int32)
    segment = positions[None, :] // slot_size
    offset = positions[None, :] - segment * slot_size
    slot_index_list = jnp.arange(lens.shape[1], dtype=jnp.int32)
    seg_len = jnp.sum(
        jnp.where(segment[:, :, None] == slot_index_list[None, None, :], lens[:, None, :], 0),
        axis=-1,
    )
    return (segment, offset < seg_len)


def block_mask(q_seg, k_seg, k_valid, causal, first_row, block_size):
    query_portion = lax.dynamic_slice_in_dim(q_seg, first_row, block_size, 1)
    q_pos = first_row + jnp.arange(block_size, dtype=jnp.int32)
    k_pos = jnp.arange(k_seg.shape[1], dtype=jnp.int32)
    order_ok = (k_pos[None, :] <= q_pos[:, None]) | jnp.logical_not(causal)
    return (query_portion[:, :, None] == k_seg[:, None, :]) & k_valid[:, None, :] & order_ok[None]


def attend_forward(q_rows, k_rows, v_rows, q_seg, k_seg, k_valid, causal):
    seq_count, row_len, feat_width = q_rows.shape
    head_count = feat_width // HD
    q_heads = q_rows.reshape(seq_count, row_len, head_count, HD)
    k_heads = k_rows.reshape(seq_count, k_rows.shape[1], head_count, HD)
    v_heads = v_rows.reshape(seq_count, v_rows.shape[1], head_count, HD)
    block_size = min(512, row_len)
    scaling = HD ** (-0.5)

    def one_block(block_num):
        first_row = block_num * block_size
        q_block = lax.dynamic_slice_in_dim(q_heads, first_row, block_size, 1)
        key_mask = block_mask(q_seg, k_seg, k_valid, causal, first_row, block_size)
        scores = (
            jnp.einsum("bqhd,bkhd->bhqk", q_block, k_heads, preferred_element_type=jnp.float32)
            * scaling
        )
        scores = jnp.where(key_mask[:, None], scores, NEG)
        top_score = jnp.max(scores, axis=-1, keepdims=True)
        expo = jnp.exp(scores - top_score)
        totals = jnp.sum(expo, axis=-1, keepdims=True)
        attn_prob = expo / totals
        result = jnp.einsum(
            "bhqk,bkhd->bqhd",
            attn_prob.astype(jnp.bfloat16),
            v_heads,
            preferred_element_type=jnp.float32,
        )
        return (result.astype(jnp.bfloat16), (top_score + jnp.log(totals))[..., 0])

    blocks_out, log_sums = lax.map(one_block, jnp.arange(row_len // block_size, dtype=jnp.int32))
    attended = jnp.moveaxis(blocks_out, 0, 1).reshape(seq_count, row_len, feat_width)
    return (attended, log_sums)


def attend_backward(q_rows, k_rows, v_rows, d_out, log_sums, q_seg, k_seg, k_valid, causal):
    seq_count, row_len, feat_width = q_rows.shape
    head_count = feat_width // HD
    q_heads = q_rows.reshape(seq_count, row_len, head_count, HD)
    k_heads = k_rows.reshape(seq_count, k_rows.shape[1], head_count, HD)
    v_heads = v_rows.reshape(seq_count, v_rows.shape[1], head_count, HD)
    d_heads = d_out.reshape(seq_count, row_len, head_count, HD)
    block_size = min(512, row_len)
    scaling = HD ** (-0.5)

    def one_block(carry, item):
        block_num, lse_block = item
        first_row = block_num * block_size
        q_block = lax.dynamic_slice_in_dim(q_heads, first_row, block_size, 1)
        d_block = lax.dynamic_slice_in_dim(d_heads, first_row, block_size, 1)
        key_mask = block_mask(q_seg, k_seg, k_valid, causal, first_row, block_size)
        scores = (
            jnp.einsum("bqhd,bkhd->bhqk", q_block, k_heads, preferred_element_type=jnp.float32)
            * scaling
        )
        scores = jnp.where(key_mask[:, None], scores, NEG)
        attn_prob = jnp.exp(scores - lse_block[..., None])
        d_prob = jnp.einsum("bqhd,bkhd->bhqk", d_block, v_heads, preferred_element_type=jnp.float32)
        row_dot = jnp.sum(d_prob * attn_prob, axis=-1, keepdims=True)
        d_scores = (attn_prob * (d_prob - row_dot)).astype(jnp.bfloat16)
        d_query = (
            jnp.einsum("bhqk,bkhd->bqhd", d_scores, k_heads, preferred_element_type=jnp.float32)
            * scaling
        ).astype(jnp.bfloat16)
        d_keys = (
            carry[0]
            + jnp.einsum("bhqk,bqhd->bkhd", d_scores, q_block, preferred_element_type=jnp.float32)
            * scaling
        )
        d_vals = carry[1] + jnp.einsum(
            "bhqk,bqhd->bkhd",
            attn_prob.astype(jnp.bfloat16),
            d_block,
            preferred_element_type=jnp.float32,
        )
        return ((d_keys, d_vals), d_query)

    zero_keys = jnp.zeros(k_heads.shape, jnp.float32)
    (d_keys, d_vals), d_queries = lax.scan(
        one_block,
        (zero_keys, zero_keys),
        (jnp.arange(row_len // block_size, dtype=jnp.int32), log_sums),
    )
    d_query_rows = jnp.moveaxis(d_queries, 0, 1).reshape(seq_count, row_len, feat_width)
    key_len = k_rows.shape[1]
    return (
        d_query_rows,
        d_keys.reshape(seq_count, key_len, feat_width).astype(jnp.bfloat16),
        d_vals.reshape(seq_count, key_len, feat_width).astype(jnp.bfloat16),
    )


def body(
    inputs,
    cotangent,
    lengths,
    row_flags,
    qkv_w,
    out_w,
    cross_w,
    up_w,
    down_w,
    norm_gain,
    norm_bias,
    cross_gain,
    cross_bias,
):
    is_dec = lax.axis_index("section") == 1
    per_batch = inputs.shape[1] // MB
    shard_len = inputs.shape[2]
    w_qkv = qkv_w[0]
    w_out = out_w[0]
    w_cross = cross_w[0]
    w_up = up_w[0]
    w_down = down_w[0]
    gains = jnp.where(is_dec, norm_gain[1], norm_gain[0])
    biases = jnp.where(is_dec, norm_bias[1], norm_bias[0])

    def clamp_batch(batch_num):
        return min(max(batch_num, 0), MB - 1)

    def rows_of(array, batch_num):
        chosen = clamp_batch(batch_num)
        return array[0, chosen * per_batch : (chosen + 1) * per_batch].astype(jnp.float32)

    def picked(array, enc_num, dec_num):
        return jnp.where(is_dec, rows_of(array, dec_num), rows_of(array, enc_num))

    def side_info(side, batch_num):
        chosen = clamp_batch(batch_num)
        return row_info(
            lengths[side, chosen * per_batch : (chosen + 1) * per_batch],
            row_flags[chosen * per_batch : (chosen + 1) * per_batch],
        )

    saved = []
    finals = []
    memory_rows = jnp.zeros((per_batch, shard_len, inputs.shape[3]), jnp.float32)
    for tick_num in range(MB + 1):
        masks_dec_num = tick_num - 1
        src_enc = side_info(0, tick_num)
        tgt_dec = side_info(1, masks_dec_num)
        src_dec = side_info(0, masks_dec_num)
        own_seg = jnp.where(is_dec, tgt_dec[0], src_enc[0])
        own_valid = jnp.where(is_dec, tgt_dec[1], src_enc[1])
        own_seg, own_valid, cross_qseg, cross_kseg, cross_kvalid = (
            own_seg,
            own_valid,
            tgt_dec[0],
            src_dec[0],
            src_dec[1],
        )
        layer_in = picked(inputs, tick_num, tick_num - 1)
        x_gath = spread_first(layer_in.astype(jnp.bfloat16))
        qkv_rows = jnp.einsum(
            "bld,cde->cble", x_gath, w_qkv, preferred_element_type=jnp.float32
        ).astype(jnp.bfloat16)
        self_att, self_lse = attend_forward(
            qkv_rows[0], qkv_rows[1], qkv_rows[2], own_seg, own_seg, own_valid, is_dec
        )
        self_branch = collect(
            jnp.einsum("ble,ed->bld", self_att, w_out, preferred_element_type=jnp.float32)
        )
        mid_rows, normed_one, inverse_one = layer_norm(layer_in + self_branch, gains[0], biases[0])
        feed_rows = jnp.where(is_dec, mid_rows, memory_rows)
        feed_gath = spread_next(feed_rows.astype(jnp.bfloat16))
        projected = jnp.einsum(
            "bld,cde->cble", feed_gath, w_cross, preferred_element_type=jnp.float32
        ).astype(jnp.bfloat16)
        received = passed_along(projected, "section", 1)
        cross_att, cross_lse = attend_forward(
            projected[0], received[0], received[1], cross_qseg, cross_kseg, cross_kvalid, False
        )
        cross_branch = collect(
            jnp.einsum("ble,de->bld", cross_att, w_cross[1], preferred_element_type=jnp.float32)
        )
        cross_rows, normed_two, inverse_two = layer_norm(
            mid_rows + cross_branch, cross_gain, cross_bias
        )
        ffn_in = jnp.where(is_dec, cross_rows, mid_rows)
        ffn_gath = spread_next(ffn_in.astype(jnp.bfloat16))
        hidden = jnp.einsum("bld,df->blf", ffn_gath, w_up, preferred_element_type=jnp.float32)
        activ = jax.nn.silu(hidden).astype(jnp.bfloat16)
        ffn_branch = collect(
            jnp.einsum("blf,fd->bld", activ, w_down, preferred_element_type=jnp.float32)
        )
        layer_out, normed_three, inverse_three = layer_norm(
            ffn_in + ffn_branch, gains[1], biases[1]
        )
        finals.append(layer_out)
        memory_rows = layer_out
        saved.append(
            {
                "x_gath": x_gath,
                "qkv_rows": qkv_rows,
                "self_att": self_att,
                "self_lse": self_lse,
                "normed_one": normed_one,
                "inverse_one": inverse_one,
                "feed_gath": feed_gath,
                "projected": projected,
                "received": received,
                "cross_att": cross_att,
                "cross_lse": cross_lse,
                "normed_two": normed_two,
                "inverse_two": inverse_two,
                "ffn_gath": ffn_gath,
                "hidden": hidden,
                "normed_three": normed_three,
                "inverse_three": inverse_three,
                "own_seg": own_seg,
                "own_valid": own_valid,
                "cross_qseg": cross_qseg,
                "cross_kseg": cross_kseg,
                "cross_kvalid": cross_kvalid,
            }
        )
    acc_qkv = jnp.zeros(w_qkv.shape, jnp.float32)
    acc_out = jnp.zeros(w_out.shape, jnp.float32)
    acc_cross = jnp.zeros(w_cross.shape, jnp.float32)
    acc_up = jnp.zeros(w_up.shape, jnp.float32)
    acc_down = jnp.zeros(w_down.shape, jnp.float32)
    acc_gain = jnp.zeros(gains.shape, jnp.float32)
    acc_bias = jnp.zeros(gains.shape, jnp.float32)
    acc_cgain = jnp.zeros(cross_gain.shape, jnp.float32)
    acc_cbias = jnp.zeros(cross_gain.shape, jnp.float32)
    d_memory = jnp.zeros((per_batch, shard_len, inputs.shape[3]), jnp.float32)
    input_grads = []
    for back_tick in range(MB + 1):
        record = saved[MB - back_tick]
        main_on = jnp.where(is_dec, 1.0 if back_tick < MB else 0.0, 1.0 if back_tick >= 1 else 0.0)
        cross_on = 1.0 if back_tick < MB else 0.0
        dec_on = jnp.where(is_dec, cross_on, 0.0)
        grad_out = picked(cotangent, MB - back_tick, MB - 1 - back_tick) + jnp.where(
            is_dec, 0.0, d_memory
        )
        d_resid_three, d_gain_three, d_bias_three = norm_back(
            grad_out, record["normed_three"], record["inverse_three"], gains[1]
        )
        d_ffn_gath = spread_grad(d_resid_three.astype(jnp.bfloat16))
        hidden = record["hidden"]
        activ = jax.nn.silu(hidden).astype(jnp.bfloat16)
        g_down = jnp.einsum("blf,bld->fd", activ, d_ffn_gath, preferred_element_type=jnp.float32)
        d_activ = jnp.einsum("bld,fd->blf", d_ffn_gath, w_down, preferred_element_type=jnp.float32)
        sigm = jax.nn.sigmoid(hidden)
        d_hidden = (d_activ * sigm * (1.0 + hidden * (1.0 - sigm))).astype(jnp.bfloat16)
        g_up = jnp.einsum(
            "bld,blf->df", record["ffn_gath"], d_hidden, preferred_element_type=jnp.float32
        )
        d_ffn_in = d_resid_three + collect_grad(
            jnp.einsum("blf,df->bld", d_hidden, w_up, preferred_element_type=jnp.float32)
        )
        d_resid_two, d_cgain, d_cbias = norm_back(
            d_ffn_in, record["normed_two"], record["inverse_two"], cross_gain
        )
        d_cross_gath = spread_grad(d_resid_two.astype(jnp.bfloat16))
        g_cross_out = jnp.einsum(
            "bld,ble->de", d_cross_gath, record["cross_att"], preferred_element_type=jnp.float32
        )
        d_cross_att = jnp.einsum(
            "bld,de->ble", d_cross_gath, w_cross[1], preferred_element_type=jnp.float32
        ).astype(jnp.bfloat16)
        projected = record["projected"]
        received = record["received"]
        d_cq, d_ck, d_cv = attend_backward(
            projected[0],
            received[0],
            received[1],
            d_cross_att,
            record["cross_lse"],
            record["cross_qseg"],
            record["cross_kseg"],
            record["cross_kvalid"],
            False,
        )
        returned = passed_along(jnp.stack([d_ck, d_cv]), "section", -1)
        first_grad = jnp.where(is_dec, d_cq, returned[0])
        second_grad = jnp.where(is_dec, jnp.zeros_like(returned[1]), returned[1])
        feed_gath = record["feed_gath"]
        g_cross_zero = jnp.einsum(
            "bld,ble->de", feed_gath, first_grad, preferred_element_type=jnp.float32
        )
        g_cross_one = jnp.where(
            is_dec,
            g_cross_out,
            jnp.einsum("bld,ble->de", feed_gath, second_grad, preferred_element_type=jnp.float32),
        )
        d_feed_part = jnp.einsum(
            "ble,de->bld", first_grad, w_cross[0], preferred_element_type=jnp.float32
        )
        d_feed_part = d_feed_part + jnp.einsum(
            "ble,de->bld", second_grad, w_cross[1], preferred_element_type=jnp.float32
        )
        d_feed = collect_grad(d_feed_part)
        d_memory = d_feed
        d_mid = jnp.where(is_dec, d_resid_two + d_feed, d_ffn_in)
        d_resid_one, d_gain_one, d_bias_one = norm_back(
            d_mid, record["normed_one"], record["inverse_one"], gains[0]
        )
        d_self_gath = spread_grad(d_resid_one.astype(jnp.bfloat16))
        g_out = jnp.einsum(
            "ble,bld->ed", record["self_att"], d_self_gath, preferred_element_type=jnp.float32
        )
        d_self_att = jnp.einsum(
            "bld,ed->ble", d_self_gath, w_out, preferred_element_type=jnp.float32
        ).astype(jnp.bfloat16)
        qkv_rows = record["qkv_rows"]
        d_query, d_key, d_val = attend_backward(
            qkv_rows[0],
            qkv_rows[1],
            qkv_rows[2],
            d_self_att,
            record["self_lse"],
            record["own_seg"],
            record["own_seg"],
            record["own_valid"],
            is_dec,
        )
        d_stack = jnp.stack([d_query, d_key, d_val])
        g_qkv = jnp.einsum(
            "bld,cble->cde", record["x_gath"], d_stack, preferred_element_type=jnp.float32
        )
        d_layer_in = d_resid_one + collect_grad(
            jnp.einsum("cble,cde->bld", d_stack, w_qkv, preferred_element_type=jnp.float32)
        )
        input_grads.append(d_layer_in)
        tick_terms = (
            main_on * g_qkv,
            main_on * g_out,
            cross_on * jnp.stack([g_cross_zero, g_cross_one]),
            main_on * g_up,
            main_on * g_down,
        )
        acc_qkv = acc_qkv + tick_terms[0]
        acc_out = acc_out + tick_terms[1]
        acc_cross = acc_cross + tick_terms[2]
        acc_up = acc_up + tick_terms[3]
        acc_down = acc_down + tick_terms[4]
        acc_gain = acc_gain + main_on * jnp.stack([d_gain_one, d_gain_three])
        acc_bias = acc_bias + main_on * jnp.stack([d_bias_one, d_bias_three])
        acc_cgain = acc_cgain + dec_on * d_cgain
        acc_cbias = acc_cbias + dec_on * d_cbias
    acc_qkv, acc_out, acc_cross, acc_up, acc_down = (
        lax.psum(acc_qkv.astype(jnp.bfloat16), "dp").astype(jnp.float32),
        lax.psum(acc_out.astype(jnp.bfloat16), "dp").astype(jnp.float32),
        lax.psum(acc_cross.astype(jnp.bfloat16), "dp").astype(jnp.float32),
        lax.psum(acc_up.astype(jnp.bfloat16), "dp").astype(jnp.float32),
        lax.psum(acc_down.astype(jnp.bfloat16), "dp").astype(jnp.float32),
    )
    zero_pair = jnp.zeros(acc_gain.shape, jnp.float32)
    full_gain = jnp.where(
        is_dec, jnp.stack([zero_pair, acc_gain]), jnp.stack([acc_gain, zero_pair])
    )
    full_bias = jnp.where(
        is_dec, jnp.stack([zero_pair, acc_bias]), jnp.stack([acc_bias, zero_pair])
    )
    full_gain, full_bias, acc_cgain, acc_cbias = lax.psum(
        (full_gain, full_bias, acc_cgain, acc_cbias), ("section", "dp", "tensor")
    )
    out_rows = jnp.concatenate(
        [jnp.where(is_dec, finals[batch_num + 1], finals[batch_num]) for batch_num in range(MB)],
        axis=0,
    )
    grad_rows = jnp.concatenate(
        [
            jnp.where(is_dec, input_grads[MB - 1 - batch_num], input_grads[MB - batch_num])
            for batch_num in range(MB)
        ],
        axis=0,
    )
    return (
        out_rows.astype(jnp.bfloat16)[None],
        grad_rows[None],
        acc_qkv[None],
        acc_out[None],
        acc_cross[None],
        acc_up[None],
        acc_down[None],
        full_gain,
        full_bias,
        acc_cgain,
        acc_cbias,
    )


def solution(mesh):
    return jax.shard_map(
        body,
        mesh=mesh,
        in_specs=(
            P("section", "dp", "tensor", None),
            P("section", "dp", "tensor", None),
            P(None, "dp", None),
            P("dp"),
            P("section", None, None, "tensor"),
            P("section", "tensor", None),
            P("section", None, None, "tensor"),
            P("section", None, "tensor"),
            P("section", "tensor", None),
            P(),
            P(),
            P(),
            P(),
        ),
        out_specs=(
            P("section", "dp", "tensor", None),
            P("section", "dp", "tensor", None),
            P("section", None, None, "tensor"),
            P("section", "tensor", None),
            P("section", None, None, "tensor"),
            P("section", None, "tensor"),
            P("section", "tensor", None),
            P(),
            P(),
            P(),
            P(),
        ),
        check_vma=False,
    )
```

profile of v0, /device:TPU:9, one launch (start us, length us, event | category | flops | bytes accessed | tf_op | source)
XLA Modules:
  0.0 1433.5 jit_solution(13545351658995155410)
XLA Ops:
  15.4 23.7 %all-gather.55.cloned.1.call-done = bf16[1,1,1024,512]{3,2,1,0:T(8,128)(2,1)} async-done(((bf16[1,1,256,512]{3,2,1,0:T(8,128)(2,1)}), bf16[1,1,1024,512]{3,2,1,0:T(8,128)(2,1)}) %all-gather.55.cloned.1.call-update) | async-done | bytes 1048592 | tf_op jit(solution)/shard_map/all_gather | solution.py:23
  41.1 27.6 %all-gather.53.cloned.1.call-done = bf16[1,1,1024,512]{3,2,1,0:T(8,128)(2,1)} async-done(((bf16[1,1,256,512]{3,2,1,0:T(8,128)(2,1)}), bf16[1,1,1024,512]{3,2,1,0:T(8,128)(2,1)}) %all-gather.53.cloned.1.call-update) | async-done | bytes 1048592 | tf_op jit(solution)/shard_map/all_gather | solution.py:23
  110.8 26.9 %reduce-scatter.31.cloned.1.call-done = bf16[1,256,512]{2,1,0:T(8,128)(2,1)} async-done(((bf16[1,1024,512]{2,1,0:T(8,128)(2,1)}), bf16[1,256,512]{2,1,0:T(8,128)(2,1)}) %reduce-scatter.31.cloned.1.call-update) | async-done | bytes 262160 | tf_op jit(solution)/shard_map/reduce_scatter | solution.py:31
  143.6 25.7 %all-gather.23.cloned.1.call-done = bf16[1,1024,512]{2,1,0:T(8,128)(2,1)} async-done(((bf16[1,256,512]{2,1,0:T(8,128)(2,1)}), bf16[1,1024,512]{2,1,0:T(8,128)(2,1)}) %all-gather.23.cloned.1.call-update) | async-done | bytes 1048592 | tf_op jit(solution)/shard_map/all_gather | solution.py:27
  175.9 22.9 %all-gather.21.cloned.1.call-done = bf16[1,1024,512]{2,1,0:T(8,128)(2,1)} async-done(((bf16[1,256,512]{2,1,0:T(8,128)(2,1)}), bf16[1,1024,512]{2,1,0:T(8,128)(2,1)}) %all-gather.21.cloned.1.call-update) | async-done | bytes 1048592 | tf_op jit(solution)/shard_map/all_gather | solution.py:23
  240.5 28.8 %reduce-scatter.23.cloned.1.call-done = bf16[1,256,512]{2,1,0:T(8,128)(2,1)} async-done(((bf16[1,1024,512]{2,1,0:T(8,128)(2,1)}), bf16[1,256,512]{2,1,0:T(8,128)(2,1)}) %reduce-scatter.23.cloned.1.call-update) | async-done | bytes 262160 | tf_op jit(solution)/shard_map/reduce_scatter | solution.py:31
  274.5 28.4 %all-gather.25.cloned.1.call-done = bf16[1,1024,512]{2,1,0:T(8,128)(2,1)} async-done(((bf16[1,256,512]{2,1,0:T(8,128)(2,1)}), bf16[1,1024,512]{2,1,0:T(8,128)(2,1)}) %all-gather.25.cloned.1.call-update) | async-done | bytes 1048592 | tf_op jit(solution)/shard_map/all_gather | solution.py:27
  308.0 25.0 %reduce-scatter.25.cloned.1.call-done = bf16[1,256,512]{2,1,0:T(8,128)(2,1)} async-done(((bf16[1,1024,512]{2,1,0:T(8,128)(2,1)}), bf16[1,256,512]{2,1,0:T(8,128)(2,1)}) %reduce-scatter.25.cloned.1.call-update) | async-done | bytes 262160 | tf_op jit(solution)/shard_map/reduce_scatter | solution.py:31
  336.7 28.4 %all-gather.27.cloned.1.call-done = bf16[1,1024,512]{2,1,0:T(8,128)(2,1)} async-done(((bf16[1,256,512]{2,1,0:T(8,128)(2,1)}), bf16[1,1024,512]{2,1,0:T(8,128)(2,1)}) %all-gather.27.cloned.1.call-update) | async-done | bytes 1048592 | tf_op jit(solution)/shard_map/all_gather | solution.py:27
  399.9 27.4 %reduce-scatter.27.cloned.1.call-done = bf16[1,256,512]{2,1,0:T(8,128)(2,1)} async-done(((bf16[1,1024,512]{2,1,0:T(8,128)(2,1)}), bf16[1,256,512]{2,1,0:T(8,128)(2,1)}) %reduce-scatter.27.cloned.1.call-update) | async-done | bytes 262160 | tf_op jit(solution)/shard_map/reduce_scatter | solution.py:31
  429.8 28.4 %all-gather.29.cloned.1.call-done = bf16[1,1024,512]{2,1,0:T(8,128)(2,1)} async-done(((bf16[1,256,512]{2,1,0:T(8,128)(2,1)}), bf16[1,1024,512]{2,1,0:T(8,128)(2,1)}) %all-gather.29.cloned.1.call-update) | async-done | bytes 1048592 | tf_op jit(solution)/shard_map/all_gather | solution.py:27
  463.5 25.0 %reduce-scatter.29.cloned.1.call-done = bf16[1,256,512]{2,1,0:T(8,128)(2,1)} async-done(((bf16[1,1024,512]{2,1,0:T(8,128)(2,1)}), bf16[1,256,512]{2,1,0:T(8,128)(2,1)}) %reduce-scatter.29.cloned.1.call-update) | async-done | bytes 262160 | tf_op jit(solution)/shard_map/reduce_scatter | solution.py:31
  493.8 28.5 %all-gather.31.cloned.1.call-done = bf16[1,1024,512]{2,1,0:T(8,128)(2,1)} async-done(((bf16[1,256,512]{2,1,0:T(8,128)(2,1)}), bf16[1,1024,512]{2,1,0:T(8,128)(2,1)}) %all-gather.31.cloned.1.call-update) | async-done | bytes 1048592 | tf_op jit(solution)/shard_map/all_gather | solution.py:27
  557.3 27.1 %reduce-scatter.33.cloned.1.call-done = bf16[1,256,512]{2,1,0:T(8,128)(2,1)} async-done(((bf16[1,1024,512]{2,1,0:T(8,128)(2,1)}), bf16[1,256,512]{2,1,0:T(8,128)(2,1)}) %reduce-scatter.33.cloned.1.call-update) | async-done | bytes 262160 | tf_op jit(solution)/shard_map/reduce_scatter | solution.py:31
  588.9 28.5 %all-gather.33.cloned.1.call-done = bf16[1,1024,512]{2,1,0:T(8,128)(2,1)} async-done(((bf16[1,256,512]{2,1,0:T(8,128)(2,1)}), bf16[1,1024,512]{2,1,0:T(8,128)(2,1)}) %all-gather.33.cloned.1.call-update) | async-done | bytes 1048592 | tf_op jit(solution)/shard_map/all_gather | solution.py:27
  622.6 25.0 %reduce-scatter.35.cloned.1.call-done = bf16[1,256,512]{2,1,0:T(8,128)(2,1)} async-done(((bf16[1,1024,512]{2,1,0:T(8,128)(2,1)}), bf16[1,256,512]{2,1,0:T(8,128)(2,1)}) %reduce-scatter.35.cloned.1.call-update) | async-done | bytes 262160 | tf_op jit(solution)/shard_map/reduce_scatter | solution.py:31
  653.2 28.4 %all-gather.35.cloned.1.call-done = bf16[1,1024,512]{2,1,0:T(8,128)(2,1)} async-done(((bf16[1,256,512]{2,1,0:T(8,128)(2,1)}), bf16[1,1024,512]{2,1,0:T(8,128)(2,1)}) %all-gather.35.cloned.1.call-update) | async-done | bytes 1048592 | tf_op jit(solution)/shard_map/all_gather | solution.py:37
  687.6 25.0 %reduce-scatter.37.cloned.1.call-done = bf16[1,256,512]{2,1,0:T(8,128)(2,1)} async-done(((bf16[1,1024,512]{2,1,0:T(8,128)(2,1)}), bf16[1,256,512]{2,1,0:T(8,128)(2,1)}) %reduce-scatter.37.cloned.1.call-update) | async-done | bytes 262160 | tf_op jit(solution)/shard_map/reduce_scatter | solution.py:41
  717.9 28.4 %all-gather.37.cloned.1.call-done = bf16[1,1024,512]{2,1,0:T(8,128)(2,1)} async-done(((bf16[1,256,512]{2,1,0:T(8,128)(2,1)}), bf16[1,1024,512]{2,1,0:T(8,128)(2,1)}) %all-gather.37.cloned.1.call-update) | async-done | bytes 1048592 | tf_op jit(solution)/shard_map/all_gather | solution.py:37
  791.6 25.3 %reduce-scatter.39.cloned.1.call-done = bf16[1,256,512]{2,1,0:T(8,128)(2,1)} async-done(((bf16[1,1024,512]{2,1,0:T(8,128)(2,1)}), bf16[1,256,512]{2,1,0:T(8,128)(2,1)}) %reduce-scatter.39.cloned.1.call-update) | async-done | bytes 262160 | tf_op jit(solution)/shard_map/reduce_scatter | solution.py:41
  820.6 28.5 %all-gather.39.cloned.1.call-done = bf16[1,1024,512]{2,1,0:T(8,128)(2,1)} async-done(((bf16[1,256,512]{2,1,0:T(8,128)(2,1)}), bf16[1,1024,512]{2,1,0:T(8,128)(2,1)}) %all-gather.39.cloned.1.call-update) | async-done | bytes 1048592 | tf_op jit(solution)/shard_map/all_gather | solution.py:37
  856.0 25.0 %reduce-scatter.41.cloned.1.call-done = bf16[1,256,512]{2,1,0:T(8,128)(2,1)} async-done(((bf16[1,1024,512]{2,1,0:T(8,128)(2,1)}), bf16[1,256,512]{2,1,0:T(8,128)(2,1)}) %reduce-scatter.41.cloned.1.call-update) | async-done | bytes 262160 | tf_op jit(solution)/shard_map/reduce_scatter | solution.py:41
  885.0 28.4 %all-gather.41.cloned.1.call-done = bf16[1,1024,512]{2,1,0:T(8,128)(2,1)} async-done(((bf16[1,256,512]{2,1,0:T(8,128)(2,1)}), bf16[1,1024,512]{2,1,0:T(8,128)(2,1)}) %all-gather.41.cloned.1.call-update) | async-done | bytes 1048592 | tf_op jit(solution)/shard_map/all_gather | solution.py:37
  955.2 24.9 %reduce-scatter.43.cloned.1.call-done = bf16[1,256,512]{2,1,0:T(8,128)(2,1)} async-done(((bf16[1,1024,512]{2,1,0:T(8,128)(2,1)}), bf16[1,256,512]{2,1,0:T(8,128)(2,1)}) %reduce-scatter.43.cloned.1.call-update) | async-done | bytes 262160 | tf_op jit(solution)/shard_map/reduce_scatter | solution.py:41
  985.6 28.4 %all-gather.45.cloned.1.call-done = bf16[1,1024,512]{2,1,0:T(8,128)(2,1)} async-done(((bf16[1,256,512]{2,1,0:T(8,128)(2,1)}), bf16[1,1024,512]{2,1,0:T(8,128)(2,1)}) %all-gather.45.cloned.1.call-update) | async-done | bytes 1048592 | tf_op jit(solution)/shard_map/all_gather | solution.py:37
  1021.0 25.0 %reduce-scatter.47.cloned.1.call-done = bf16[1,256,512]{2,1,0:T(8,128)(2,1)} async-done(((bf16[1,1024,512]{2,1,0:T(8,128)(2,1)}), bf16[1,256,512]{2,1,0:T(8,128)(2,1)}) %reduce-scatter.47.cloned.1.call-update) | async-done | bytes 262160 | tf_op jit(solution)/shard_map/reduce_scatter | solution.py:41
  1051.7 28.4 %all-gather.47.cloned.1.call-done = bf16[1,1024,512]{2,1,0:T(8,128)(2,1)} async-done(((bf16[1,256,512]{2,1,0:T(8,128)(2,1)}), bf16[1,1024,512]{2,1,0:T(8,128)(2,1)}) %all-gather.47.cloned.1.call-update) | async-done | bytes 1048592 | tf_op jit(solution)/shard_map/all_gather | solution.py:37
  1082.5 20.1 %while.189 = (s32[]{:T(128)}, f32[1,1024,2,64]{1,3,2,0:T(8,128)S(1)}, f32[1,1024,2,64]{1,3,2,0:T(8,128)}, bf16[2,1,512,2,64]{2,4,3,1,0:T(8,128)(2,1)}, s32[2]{0:...) while((s32[]{:T(128)}, ...), condition=%wide.region_86.88_spmd.clone, body=%wide.region_84.87_spmd.clone.sunk | while | flops 688651264 | bytes 45524396 | solution.py:162
  1123.6 25.2 %reduce-scatter.49.cloned.1.call-done = bf16[1,256,512]{2,1,0:T(8,128)(2,1)} async-done(((bf16[1,1024,512]{2,1,0:T(8,128)(2,1)}), bf16[1,256,512]{2,1,0:T(8,128)(2,1)}) %reduce-scatter.49.cloned.1.call-update) | async-done | bytes 262160 | tf_op jit(solution)/shard_map/reduce_scatter | solution.py:41
  1159.0 23.1 %all-gather.49.cloned.1.call-done = bf16[1,1024,512]{2,1,0:T(8,128)(2,1)} async-done(((bf16[1,256,512]{2,1,0:T(8,128)(2,1)}), bf16[1,1024,512]{2,1,0:T(8,128)(2,1)}) %all-gather.49.cloned.1.call-update) | async-done | bytes 1048592 | tf_op jit(solution)/shard_map/all_gather | solution.py:37
  1185.2 21.0 %while.190 = (s32[]{:T(128)}, f32[1,1024,2,64]{1,3,2,0:T(8,128)S(1)}, f32[1,1024,2,64]{1,3,2,0:T(8,128)}, bf16[2,1,512,2,64]{2,4,3,1,0:T(8,128)(2,1)}, s32[2]{0:...) while((s32[]{:T(128)}, ...), condition=%wide.region_92.94_spmd.clone, body=%wide.region_90.93_spmd.clone.sunk | while | flops 690224640 | bytes 45528624 | solution.py:162
  1350.0 41.1 %all-reduce.4 = (f32[2,2,512]{2,1,0:T(2,128)}, f32[2,2,512]{2,1,0:T(2,128)}, f32[512]{0:T(512)}, f32[512]{0:T(512)}) all-reduce(f32[2,2,512]{2,1,0:T(2,128)S(1)} %get-tuple-element.2031, f32[2,2,512]{2,1,0:T(2,128)S(1)} %get-tuple-element.2030, ...), channel_id=1, replica_groups=mesh['section'=2,'dp'=4,'tensor'=4] {'section','dp','tensor'}, use_global_device_ids=true, to_apply=%region_111.113 | all-reduce | flops 5120 | bytes 40960 | tf_op jit(solution)/shard_map/psum | solution.py:440
  (1157 shorter events, 733.1 us)
Async XLA Ops:
  9.2 59.4 %all-gather.53.cloned.1.call-start = ((), (), s32[]{:S(2)}) async-start(), calls=%async_computation.52 | async-start | bytes 1310720 | tf_op jit(solution)/shard_map/all_gather | solution.py:23
  10.0 99.1 %reduce-scatter.21.cloned.1.call-start = ((), (), s32[]{:S(2)}) async-start(), calls=%async_computation.20 | async-start | bytes 1310720 | tf_op jit(solution)/shard_map/reduce_scatter | solution.py:31
  97.9 71.5 %all-gather.23.cloned.1.call-start = ((), (), s32[]{:S(2)}) async-start(), calls=%async_computation.21 | async-start | bytes 1310720 | tf_op jit(solution)/shard_map/all_gather | solution.py:27
  140.9 57.9 %all-gather.21.cloned.1.call-start = ((), (), s32[]{:S(2)}) async-start(), calls=%async_computation.18 | async-start | bytes 1310720 | tf_op jit(solution)/shard_map/all_gather | solution.py:23
  141.5 99.1 %reduce-scatter.19.cloned.1.call-start = ((), (), s32[]{:S(2)}) async-start(), calls=%async_computation.19 | async-start | bytes 1310720 | tf_op jit(solution)/shard_map/reduce_scatter | solution.py:31
  234.7 68.2 %all-gather.25.cloned.1.call-start = ((), (), s32[]{:S(2)}) async-start(), calls=%async_computation.23 | async-start | bytes 1310720 | tf_op jit(solution)/shard_map/all_gather | solution.py:27
  274.5 58.5 %reduce-scatter.25.cloned.1.call-start = ((), (), s32[]{:S(2)}) async-start(), calls=%async_computation.24 | async-start | bytes 1310720 | tf_op jit(solution)/shard_map/reduce_scatter | solution.py:31
  336.7 90.6 %reduce-scatter.27.cloned.1.call-start = ((), (), s32[]{:S(2)}) async-start(), calls=%async_computation.26 | async-start | bytes 1310720 | tf_op jit(solution)/shard_map/reduce_scatter | solution.py:31
  399.9 58.4 %all-gather.29.cloned.1.call-start = ((), (), s32[]{:S(2)}) async-start(), calls=%async_computation.27 | async-start | bytes 1310720 | tf_op jit(solution)/shard_map/all_gather | solution.py:27
  429.8 58.7 %reduce-scatter.29.cloned.1.call-start = ((), (), s32[]{:S(2)}) async-start(), calls=%async_computation.28 | async-start | bytes 1310720 | tf_op jit(solution)/shard_map/reduce_scatter | solution.py:31
  463.4 58.8 %all-gather.31.cloned.1.call-start = ((), (), s32[]{:S(2)}) async-start(), calls=%async_computation.30 | async-start | bytes 1310720 | tf_op jit(solution)/shard_map/all_gather | solution.py:27
  493.7 90.6 %reduce-scatter.33.cloned.1.call-start = ((), (), s32[]{:S(2)}) async-start(), calls=%async_computation.31 | async-start | bytes 1310720 | tf_op jit(solution)/shard_map/reduce_scatter | solution.py:31
  557.0 60.3 %all-gather.33.cloned.1.call-start = ((), (), s32[]{:S(2)}) async-start(), calls=%async_computation.32 | async-start | bytes 1310720 | tf_op jit(solution)/shard_map/all_gather | solution.py:27
  588.9 58.7 %reduce-scatter.35.cloned.1.call-start = ((), (), s32[]{:S(2)}) async-start(), calls=%async_computation.33 | async-start | bytes 1310720 | tf_op jit(solution)/shard_map/reduce_scatter | solution.py:31
  622.5 59.2 %all-gather.35.cloned.1.call-start = ((), (), s32[]{:S(2)}) async-start(), calls=%async_computation.34 | async-start | bytes 1310720 | tf_op jit(solution)/shard_map/all_gather | solution.py:37
  653.2 59.4 %reduce-scatter.37.cloned.1.call-start = ((), (), s32[]{:S(2)}) async-start(), calls=%async_computation.35 | async-start | bytes 1310720 | tf_op jit(solution)/shard_map/reduce_scatter | solution.py:41
  687.5 58.7 %all-gather.37.cloned.1.call-start = ((), (), s32[]{:S(2)}) async-start(), calls=%async_computation.36 | async-start | bytes 1310720 | tf_op jit(solution)/shard_map/all_gather | solution.py:37
  717.8 99.1 %reduce-scatter.39.cloned.1.call-start = ((), (), s32[]{:S(2)}) async-start(), calls=%async_computation.37 | async-start | bytes 1310720 | tf_op jit(solution)/shard_map/reduce_scatter | solution.py:41
  791.5 57.5 %all-gather.39.cloned.1.call-start = ((), (), s32[]{:S(2)}) async-start(), calls=%async_computation.38 | async-start | bytes 1310720 | tf_op jit(solution)/shard_map/all_gather | solution.py:37
  820.5 60.5 %reduce-scatter.41.cloned.1.call-start = ((), (), s32[]{:S(2)}) async-start(), calls=%async_computation.39 | async-start | bytes 1310720 | tf_op jit(solution)/shard_map/reduce_scatter | solution.py:41
  856.0 57.5 %all-gather.41.cloned.1.call-start = ((), (), s32[]{:S(2)}) async-start(), calls=%async_computation.40 | async-start | bytes 1310720 | tf_op jit(solution)/shard_map/all_gather | solution.py:37
  884.9 95.2 %reduce-scatter.43.cloned.1.call-start = ((), (), s32[]{:S(2)}) async-start(), calls=%async_computation.41 | async-start | bytes 1310720 | tf_op jit(solution)/shard_map/reduce_scatter | solution.py:41
  954.7 59.3 %all-gather.45.cloned.1.call-start = ((), (), s32[]{:S(2)}) async-start(), calls=%async_computation.44 | async-start | bytes 1310720 | tf_op jit(solution)/shard_map/all_gather | solution.py:37
  985.5 60.5 %reduce-scatter.47.cloned.1.call-start = ((), (), s32[]{:S(2)}) async-start(), calls=%async_computation.45 | async-start | bytes 1310720 | tf_op jit(solution)/shard_map/reduce_scatter | solution.py:41
  1021.0 59.1 %all-gather.47.cloned.1.call-start = ((), (), s32[]{:S(2)}) async-start(), calls=%async_computation.46 | async-start | bytes 1310720 | tf_op jit(solution)/shard_map/all_gather | solution.py:37
  1051.6 97.2 %reduce-scatter.49.cloned.1.call-start = ((), (), s32[]{:S(2)}) async-start(), calls=%async_computation.47 | async-start | bytes 1310720 | tf_op jit(solution)/shard_map/reduce_scatter | solution.py:41
  1123.4 58.7 %all-gather.49.cloned.1.call-start = ((), (), s32[]{:S(2)}) async-start(), calls=%async_computation.48 | async-start | bytes 1310720 | tf_op jit(solution)/shard_map/all_gather | solution.py:37
  1153.6 64.4 %all-gather.43.cloned.1.call-start = ((), (), s32[]{:S(2)}) async-start(), calls=%async_computation.42 | async-start | bytes 1310720 | tf_op jit(solution)/shard_map/all_gather | solution.py:37
  1158.9 104.0 %reduce-scatter.51.cloned.1.call-start = ((), (), s32[]{:S(2)}) async-start(), calls=%async_computation.49 | async-start | bytes 1310720 | tf_op jit(solution)/shard_map/reduce_scatter | solution.py:41
  1217.7 58.3 %reduce-scatter.45.cloned.1.call-start = ((), (), s32[]{:S(2)}) async-start(), calls=%async_computation.43 | async-start | bytes 1310720 | tf_op jit(solution)/shard_map/reduce_scatter | solution.py:41
  1278.7 115.6 %all-reduce.8.cloned.1.call-start = ((), (), s32[]{:S(2)}) async-start(), calls=%async_computation.54 | async-start | bytes 3670016 | tf_op jit(solution)/shard_map/psum | solution.py:427
  1345.6 77.2 %reduce-scatter.53.cloned.1.call-start = ((), (), s32[]{:S(2)}) async-start(), calls=%async_computation.51 | async-start | bytes 1310720 | tf_op jit(solution)/shard_map/reduce_scatter | solution.py:41
  (285 other events, 7013.2 us)
Sparse Core Ops, SparseCore 0:
  10.2 28.8 all-gather.54
  41.2 27.4 all-gather.52
  111.9 25.8 reduce-scatter.30
  141.0 28.3 all-gather.22
  171.4 27.4 all-gather.20
  215.6 24.8 reduce-scatter.18
  243.5 25.7 reduce-scatter.22
  274.6 28.3 all-gather.24
  336.8 28.3 all-gather.26
  400.0 27.2 reduce-scatter.26
  429.9 28.3 all-gather.28
  493.9 28.3 all-gather.30
  557.2 27.1 reduce-scatter.32
  589.0 28.3 all-gather.32
  622.6 24.8 reduce-scatter.34
  653.3 28.3 all-gather.34
  687.7 24.8 reduce-scatter.36
  717.9 28.3 all-gather.36
  791.7 25.2 reduce-scatter.38
  820.6 28.3 all-gather.38
  885.0 28.3 all-gather.40
  954.9 25.2 reduce-scatter.42
  985.6 28.3 all-gather.44
  1021.1 24.8 reduce-scatter.46
  1051.7 28.3 all-gather.46
  1123.5 25.2 reduce-scatter.48
  1153.7 28.3 all-gather.48
  1183.7 27.4 all-gather.42
  1251.1 24.8 reduce-scatter.44
  1278.8 28.3 all-gather.50
  1345.7 48.5 all-reduce.7
  1397.1 25.6 reduce-scatter.52
  (5 shorter events, 124.0 us)
where the time goes:
time: 1450 us; the launch traced here: 1430 us
  waiting for transfers between devices  899 us (62%)
  matrix products  212 us (15%)
  other arithmetic  135 us (9%)
  local copies, waits for them, and re-layouts  89.7 us (6%)
  blocking collectives  41.1 us (3%)
  starting transfers between devices  19.6 us (1%)
  between operations  19.2 us (1%)
  loops' own time  17.7 us (1%)
    all_gather x9, waiting for transfers between devices, spread_grad(): return lax.all_gather(rows_low, 'tensor', axis=1, tiled=True)  211 us
    reduce_scatter x9, waiting for transfers between devices, collect(): lax.psum_scatter(partial_value.astype(jnp.bfloat16), 'tensor', scatter_di...  202 us
    reduce_scatter x9, waiting for transfers between devices, collect_grad(): lax.psum_scatter(partial_value.astype(jnp.bfloat16), 'tensor', scatter_di...  183 us
    all_gather x6, waiting for transfers between devices, spread_next(): return lax.all_gather(rows_low, 'tensor', axis=1, tiled=True)  168 us
    all_gather x3, waiting for transfers between devices, spread_first(): return lax.all_gather(rows_low, 'tensor', axis=1, tiled=True)  74.2 us
    ppermute x6, waiting for transfers between devices, passed_along(): return lax.ppermute(block, axis, route)  56.4 us
    psum x1, blocking collectives, body(): lax.psum((full_gain, full_bias, acc_cgain, acc_cbias), ('section', 'dp',...  41.1 us
    dot_general x24, matrix products, one_block(): jnp.einsum('bqhd,bkhd->bhqk', q_block, k_heads, preferred_element_type=jn...  29.6 us
  transfers between devices with their start and end apart: 43, of which 40 were waited for; matrix products, arithmetic and copies ran while one was open for 11% of the time, Pallas kernels for 0%

commit v1 on v0

v1 whole, which is shorter than its diff:
```python
import functools

import jax
import jax.numpy as jnp
from jax import lax
from jax.experimental import pallas as pl
from jax.experimental.pallas import tpu as pltpu
from jax.sharding import PartitionSpec as P

HEADS = 8
HD = 64
PAIR = 2 * HD
SLOT_BITS = 7
SLOTS = 8
NEG = -1e30
EPS = 1e-05
SCALE = HD ** -0.5
BF = jnp.bfloat16
F32 = jnp.float32
MIB = 1024 * 1024


def swap_dp(x, bit):
    n = lax.axis_size("dp")
    return lax.ppermute(x, "dp", [(i, i ^ bit) for i in range(n)])


def shift_tensor(x, step):
    n = lax.axis_size("tensor")
    return lax.ppermute(x, "tensor", [(i, (i + step) % n) for i in range(n)])


def swap_tensor(x, bit):
    n = lax.axis_size("tensor")
    return lax.ppermute(x, "tensor", [(i, i ^ bit) for i in range(n)])


def to_decoder(x):
    return lax.ppermute(x, "section", [(0, 1)])


def to_encoder(x):
    return lax.ppermute(x, "section", [(1, 0)])


def deal_route(k):
    n_t = lax.axis_size("tensor")
    route = []
    for d in range(lax.axis_size("dp")):
        group, core = divmod(d, 2)
        for t in range(n_t):
            plane = 2 * core + (t + k) % 2
            route.append((d * n_t + t, (2 * group + t // 2) * n_t + plane))
    return route


def deal(x, k):
    return lax.ppermute(x, ("dp", "tensor"), deal_route(k))


def deal_back(x, k):
    return lax.ppermute(x, ("dp", "tensor"), [(b, a) for a, b in deal_route(k)])


def gather_pieces(piece):
    along_z = jnp.stack([piece] + [shift_tensor(piece, r) for r in range(1, 4)])
    along_y = swap_dp(along_z, 2)
    return (along_z, swap_dp(along_z, 1), along_y, swap_dp(along_y, 1))


def reduce_pieces(keep, send):
    halves = (keep.astype(F32) + swap_dp(send, 1).astype(F32)).astype(BF)
    quarter = (halves[0].astype(F32) + swap_dp(halves[1], 2).astype(F32)).astype(BF)
    total = quarter[0].astype(F32)
    for r in range(1, 4):
        total = total + shift_tensor(quarter[r], -r).astype(F32)
    bit = 4
    while bit < lax.axis_size("dp"):
        total = total + swap_dp(total.astype(BF), bit).astype(F32)
        bit *= 2
    return total.astype(BF)


def spread_pieces(piece):
    along_y = jnp.stack([piece, swap_dp(piece, 2)])
    mate = swap_dp(along_y, 1)
    return jnp.stack([along_y[0], mate[0], along_y[1], mate[1]])


def dg(a, b, ca, cb):
    return lax.dot_general(a, b, (((ca,), (cb,)), ((), ())), preferred_element_type=F32)


def norm_fwd(r):
    off = r - jnp.mean(r, axis=-1, keepdims=True)
    inv = lax.rsqrt(jnp.mean(off * off, axis=-1, keepdims=True) + EPS)
    return off * inv, inv


def norm_bwd(dy, n, inv, gain):
    sc = dy * gain
    dr = inv * (
        sc
        - jnp.mean(sc, axis=-1, keepdims=True)
        - n * jnp.mean(sc * n, axis=-1, keepdims=True)
    )
    return dr, jnp.sum(dy * n, axis=0, keepdims=True), jnp.sum(dy, axis=0, keepdims=True)


def head_lanes(h):
    return (lax.broadcasted_iota(jnp.int32, (1, PAIR), 1) // HD) == h


def mask_bias(info, n_q, n_k, q_axis):
    flip = info[9]
    q_shape = (n_q, 1) if q_axis == 0 else (1, n_q)
    full = (n_q, n_k) if q_axis == 0 else (n_k, n_q)
    q_pos = lax.broadcasted_iota(jnp.int32, q_shape, q_axis) ^ flip
    seg = jnp.where(info[8] == 1, 0, q_pos >> SLOT_BITS)
    size = jnp.zeros(q_shape, jnp.int32)
    for j in range(SLOTS):
        size = size + jnp.where(seg == j, info[j], 0)
    first = seg << SLOT_BITS
    end = first + size
    end = jnp.where(info[10] == 1, jnp.minimum(end, q_pos + 1), end)
    k_pos = lax.broadcasted_iota(jnp.int32, full, 1 - q_axis) ^ flip
    return jnp.where((k_pos >= first) & (k_pos < end), 0.0, NEG)


def weights_in_order(refs, wall):
    for rel, ref in enumerate(refs):
        for z in range(ref.shape[0]):
            wall[rel, :, z * PAIR : (z + 1) * PAIR] = ref[z]


def attend_forward(q_ref, k_ref, v_ref, bias_ref, att_ref, lse_ref):
    n_q = q_ref.shape[0]

    def pair(hp, _):
        sl = pl.ds(pl.multiple_of(hp * PAIR, PAIR), PAIR)
        kp = k_ref[:, sl]
        vp = v_ref[:, sl]
        qp = q_ref[:, sl]
        out = None
        for h in range(2):
            lanes = head_lanes(h)
            s = dg(jnp.where(lanes, qp, jnp.zeros_like(qp)), kp, 1, 1) + bias_ref[...]
            top = jnp.max(s, axis=1, keepdims=True)
            e = jnp.exp(s - top)
            total = jnp.sum(e, axis=1, keepdims=True)
            o = dg(e.astype(BF), vp, 1, 0) * (1.0 / total)
            lse = jnp.broadcast_to(top + jnp.log(total), (n_q, 8))
            lse_ref[hp * 2 + h] = jnp.transpose(lse)[0:1, :]
            o = jnp.where(lanes, o, 0.0)
            out = o if out is None else out + o
        att_ref[:, sl] = out.astype(BF)
        return 0

    lax.fori_loop(0, HEADS // 2, pair, 0)


def attend_backward(info, q_ref, k_ref, v_ref, do_ref, att_ref, lse_ref, bias_ref, rd_ref, dq_ref, dk_ref, dv_ref):
    n_q = q_ref.shape[0]
    width = q_ref.shape[1]
    block = 256
    empty = info[0]
    for j in range(1, SLOTS):
        empty = empty + info[j]
    empty = empty == 0
    p_fix = jnp.where(empty, 1.0 / k_ref.shape[0], 1.0)
    s_fix = jnp.where(empty, 0.0, 1.0)
    prod = do_ref[...].astype(F32) * att_ref[...].astype(F32)
    high = prod.astype(BF)
    low = (prod - high.astype(F32)).astype(BF)
    heads = lax.broadcasted_iota(jnp.int32, (HEADS, width), 0)
    lanes_of = lax.broadcasted_iota(jnp.int32, (HEADS, width), 1) // HD
    ones = jnp.where(heads == lanes_of, 1.0, 0.0).astype(BF)
    rd = dg(ones, high, 1, 1) + dg(ones, low, 1, 1)
    for h in range(HEADS):
        rd_ref[h] = rd[h : h + 1]

    def pair(hp, _):
        sl = pl.ds(pl.multiple_of(hp * PAIR, PAIR), PAIR)
        kp = k_ref[:, sl]
        vp = v_ref[:, sl]
        k_t = jnp.transpose(kp)
        dk = dv = None
        for qi in range(n_q // block):
            qs = slice(qi * block, (qi + 1) * block)
            qp = q_ref[qs, sl]
            dop = do_ref[qs, sl]
            dqs = []
            for h in range(2):
                lanes = head_lanes(h)
                qm = jnp.where(lanes, qp, jnp.zeros_like(qp))
                dom = jnp.where(lanes, dop, jnp.zeros_like(dop))
                s = dg(kp, qm, 1, 1) + bias_ref[:, qs]
                p = jnp.exp(s - lse_ref[hp * 2 + h, :, qs])
                dp = dg(vp, dom, 1, 1)
                ds = (p * (dp - rd_ref[hp * 2 + h, :, qs])).astype(BF)
                a = dg(p.astype(BF), dom, 1, 0)
                dv = a if dv is None else dv + a
                a = dg(ds, qm, 1, 0)
                dk = a if dk is None else dk + a
                dqs.append(dg(k_t[h * HD : (h + 1) * HD], ds, 1, 0))
            dq = jnp.transpose(jnp.concatenate(dqs, axis=0))
            dq_ref[qs, sl] = (dq * (SCALE * s_fix)).astype(BF)
        dk_ref[:, sl] = (dk * s_fix).astype(BF)
        dv_ref[:, sl] = (dv * p_fix).astype(BF)
        return 0

    lax.fori_loop(0, HEADS // 2, pair, 0)


def attention_kernel(n_src, info, *refs):
    xq = refs[:n_src[0]]
    xk = refs[n_src[0] : n_src[0] + n_src[1]]
    refs = refs[n_src[0] + n_src[1] :]
    w_refs = refs[:4]
    gain, shift = refs[4:6]
    y_ref, n_ref, inv_ref, q_ref, k_ref, v_ref, att_ref, lse_ref = refs[6:14]
    wall, bias_ref = refs[14:16]
    weights_in_order(w_refs, wall)
    me = info[11]
    bias_ref[...] = mask_bias(info, q_ref.shape[0], k_ref.shape[0], 0)
    rows = xq[0][...] if len(xq) == 1 else jnp.concatenate([r[...] for r in xq], axis=0)
    rows_low = rows.astype(BF)
    q = dg(rows_low, wall[me], 1, 0).astype(BF)
    q_ref[...] = q * jnp.asarray(SCALE, BF)
    wk = wall[me ^ 1]
    wv = wall[me ^ 2]
    at = 0
    for ref in xk:
        part = ref[...]
        k_ref[at : at + ref.shape[0]] = dg(part, wk, 1, 0).astype(BF)
        v_ref[at : at + ref.shape[0]] = dg(part, wv, 1, 0).astype(BF)
        at += ref.shape[0]
    attend_forward(q_ref, k_ref, v_ref, bias_ref, att_ref, lse_ref)
    branch = dg(att_ref[...], wall[me ^ 3], 1, 1)
    n, inv = norm_fwd(rows.astype(F32) + branch)
    n_ref[...] = n
    inv_ref[...] = inv
    y_ref[...] = n * gain[...] + shift[...]


def silu_parts(u):
    sg = jax.nn.sigmoid(u)
    return u * sg, sg


def ffn_forward_kernel(x_ref, *refs):
    ups = refs[:4]
    downs = refs[4:8]
    gain, shift, y_ref, low_ref, n_ref, inv_ref = refs[8:]
    x = x_ref[...]
    low = x.astype(BF)
    acc = x
    for up, down in zip(ups, downs):
        n_z, width, feat = up.shape
        for z in range(0, n_z, 2):
            u = dg(low, up[z : z + 2].reshape(2 * width, feat), 1, 1)
            act = silu_parts(u)[0].astype(BF)
            acc = acc + dg(act, down[z : z + 2].reshape(2 * width, feat), 1, 0)
    n, inv = norm_fwd(acc)
    y = n * gain[...] + shift[...]
    y_ref[...] = y
    low_ref[...] = y.astype(BF)
    n_ref[...] = n
    inv_ref[...] = inv


def ffn_both_kernel(x_ref, cot_ref, *refs):
    ups = refs[:4]
    downs = refs[4:8]
    gain, shift, final_ref, n_ref, inv_ref, dx_ref, u_ref = refs[8:]
    x = x_ref[...]
    low = x.astype(BF)
    acc = x
    at = 0
    for up, down in zip(ups, downs):
        n_z, width, feat = up.shape
        for z in range(0, n_z, 2):
            u = dg(low, up[z : z + 2].reshape(2 * width, feat), 1, 1)
            u_ref[:, at : at + 2 * width] = u
            at += 2 * width
            act = silu_parts(u)[0].astype(BF)
            acc = acc + dg(act, down[z : z + 2].reshape(2 * width, feat), 1, 0)
    n, inv = norm_fwd(acc)
    final_ref[...] = (n * gain[...] + shift[...]).astype(BF)
    n_ref[...] = n
    inv_ref[...] = inv
    dr, _, _ = norm_bwd(cot_ref[...].astype(F32), n, inv, gain[...])
    dbr = dr.astype(BF)
    acc = dr
    at = 0
    for up, down in zip(ups, downs):
        n_z, width, feat = up.shape
        for z in range(0, n_z, 2):
            u = u_ref[:, at : at + 2 * width]
            at += 2 * width
            sg = jax.nn.sigmoid(u)
            dact = dg(dbr, down[z : z + 2].reshape(2 * width, feat), 1, 1)
            du = (dact * sg * (1.0 + u * (1.0 - sg))).astype(BF)
            acc = acc + dg(du, up[z : z + 2].reshape(2 * width, feat), 1, 0)
    dx_ref[...] = acc


def cross_backward_kernel(info, dy_ref, n_ref, inv_ref, gain, q_ref, k_ref, v_ref, att_ref, lse_ref, w0, w1, w2, w3,
                          dh_ref, dmem_own_ref, dmem_mate_ref, dbr_ref, dq_ref, dk_ref, dv_ref, dnorm_ref,
                          wall, bias_ref, rd_ref, do_ref):
    weights_in_order((w0, w1, w2, w3), wall)
    me = info[11]
    bias_ref[...] = mask_bias(info, q_ref.shape[0], k_ref.shape[0], 1)
    dr, dg_sum, db_sum = norm_bwd(dy_ref[...], n_ref[...], inv_ref[...], gain[...])
    dnorm_ref[0:1] = dg_sum
    dnorm_ref[1:2] = db_sum
    dbr = dr.astype(BF)
    dbr_ref[...] = dbr
    do_ref[...] = dg(dbr, wall[me ^ 3], 1, 0).astype(BF)
    attend_backward(info, q_ref, k_ref, v_ref, do_ref, att_ref, lse_ref, bias_ref, rd_ref, dq_ref, dk_ref, dv_ref)
    dh_ref[...] = dr + dg(dq_ref[...], wall[me], 1, 1)
    half = dmem_own_ref.shape[0]
    wk = wall[me ^ 1]
    wv = wall[me ^ 2]
    for ref, at in ((dmem_own_ref, 0), (dmem_mate_ref, half)):
        part = dg(dk_ref[at : at + half], wk, 1, 1) + dg(dv_ref[at : at + half], wv, 1, 1)
        ref[...] = part.astype(BF)


def put_matrix(keep_ref, send_ref, me, which, value):
    slot = me ^ which
    y = slot >> 1

    @pl.when(slot % 2 == 0)
    def _():
        for z in range(4):
            keep_ref[y, z] = value[:, z * PAIR : (z + 1) * PAIR]

    @pl.when(slot % 2 == 1)
    def _():
        for z in range(4):
            send_ref[y, z] = value[:, z * PAIR : (z + 1) * PAIR]


def cross_weights_kernel(info, h_ref, mem_own, mem_mate, att_ref, dbr_ref, dq_ref, dk_ref, dv_ref, keep_ref, send_ref):
    me = info[11]
    half = mem_own.shape[0]
    put_matrix(keep_ref, send_ref, me, 0, dg(h_ref[...].astype(BF), dq_ref[...], 0, 0).astype(BF))
    for which, ref in ((1, dk_ref), (2, dv_ref)):
        value = dg(mem_own[...], ref[:half], 0, 0) + dg(mem_mate[...], ref[half:], 0, 0)
        put_matrix(keep_ref, send_ref, me, which, value.astype(BF))
    put_matrix(keep_ref, send_ref, me, 3, dg(dbr_ref[...], att_ref[...], 0, 0).astype(BF))


def ffn_backward_kernel(info, x_ref, n3_ref, inv3_ref, dy_ref, gain3, dmid_ref, n1_ref, inv1_ref, gain1, *refs):
    ups = refs[:4]
    downs = refs[4:8]
    outs = refs[8:12]
    att_g = refs[12]
    keep_ref, send_ref, dr1_ref, dbr1_ref, dnorm_ref = refs[13:18]
    wall = refs[18]
    do_ref = att_g
    weights_in_order(outs, wall)
    me = info[11]
    low = x_ref[...].astype(BF)
    dr3, dg3, db3 = norm_bwd(dy_ref[...], n3_ref[...], inv3_ref[...], gain3[...])
    dbr = dr3.astype(BF)
    acc = dr3
    for rel in range(4):
        up = ups[rel]
        down = downs[rel]
        target = (keep_ref, send_ref)[rel % 2]
        n_z, width, feat = up.shape
        for z in range(0, n_z, 2):
            wu = up[z : z + 2].reshape(2 * width, feat)
            wd = down[z : z + 2].reshape(2 * width, feat)
            u_t = dg(wu, low, 1, 1)
            act_t, sg = silu_parts(u_t)
            act_t = act_t.astype(BF)
            dact_t = dg(wd, dbr, 1, 1)
            du_t = (dact_t * sg * (1.0 + u_t * (1.0 - sg))).astype(BF)
            acc = acc + dg(du_t, wu, 0, 0)
            dup = dg(du_t, low, 1, 0).astype(BF)
            ddown = dg(act_t, dbr, 1, 0).astype(BF)
            for i in range(2):
                target[rel // 2, z + i, 0] = dup[i * width : (i + 1) * width]
                target[rel // 2, z + i, 1] = ddown[i * width : (i + 1) * width]
    dmid = jnp.where(info[12] == 1, dmid_ref[...], acc)
    dr1, dg1, db1 = norm_bwd(dmid, n1_ref[...], inv1_ref[...], gain1[...])
    dr1_ref[...] = dr1
    dbr1 = dr1.astype(BF)
    dbr1_ref[...] = dbr1
    do_ref[...] = dg(dbr1, wall[me ^ 3], 1, 0).astype(BF)
    for i, row in enumerate((dg1, dg3, db1, db3)):
        dnorm_ref[i : i + 1] = row


def self_backward_kernel(info, q_ref, k_ref, v_ref, do_ref, att_ref, lse_ref, dq_ref, dk_own, dk_mate, bias_ref, rd_ref, dk_ref, dv_ref):
    bias_ref[...] = mask_bias(info, q_ref.shape[0], k_ref.shape[0], 1)
    attend_backward(info, q_ref, k_ref, v_ref, do_ref, att_ref, lse_ref, bias_ref, rd_ref, dq_ref, dk_ref, dv_ref)
    half = q_ref.shape[0]
    dk_own[0] = dk_ref[:half]
    dk_own[1] = dv_ref[:half]
    dk_mate[0] = dk_ref[half:]
    dk_mate[1] = dv_ref[half:]


def input_backward_kernel(info, x0, x1, dr_ref, dq_ref, own_ref, got_ref, att_ref, dbr_ref, w0, w1, w2, w3,
                          dx_ref, keep_ref, send_ref, wall):
    weights_in_order((w0, w1, w2, w3), wall)
    me = info[11]
    dq = dq_ref[...]
    dk = (own_ref[0].astype(F32) + got_ref[0].astype(F32)).astype(BF)
    dv = (own_ref[1].astype(F32) + got_ref[1].astype(F32)).astype(BF)
    dx = dr_ref[...] + dg(dq, wall[me], 1, 1) + dg(dk, wall[me ^ 1], 1, 1) + dg(dv, wall[me ^ 2], 1, 1)
    dx_ref[...] = dx.astype(BF)
    x = jnp.concatenate([x0[...], x1[...]], axis=0)
    for which, value in ((0, dq), (1, dk), (2, dv)):
        put_matrix(keep_ref, send_ref, me, which, dg(x, value, 0, 0).astype(BF))
    put_matrix(keep_ref, send_ref, me, 3, dg(dbr_ref[...], att_ref[...], 0, 0).astype(BF))


def call(kernel, outs, args, scratch=(), flops=0, vmem=44):
    specs = [
        pl.BlockSpec(memory_space=pltpu.SMEM if a.dtype == jnp.int32 else pltpu.VMEM) for a in args
    ]
    size = sum(a.size * a.dtype.itemsize for a in args)
    size += sum(int(jnp.dtype(dt).itemsize) * functools.reduce(lambda p, q: p * q, shape, 1) for shape, dt in outs)
    return pl.pallas_call(
        kernel,
        out_shape=tuple(jax.ShapeDtypeStruct(shape, dt) for shape, dt in outs),
        in_specs=specs,
        out_specs=tuple(pl.BlockSpec(memory_space=pltpu.VMEM) for _ in outs),
        scratch_shapes=list(scratch),
        compiler_params=pltpu.CompilerParams(vmem_limit_bytes=vmem * MIB),
        cost_estimate=pl.CostEstimate(flops=int(flops), bytes_accessed=int(size), transcendentals=0),
    )(*args)


def body(
    inputs,
    cotangent,
    lengths,
    row_flags,
    qkv_w,
    out_w,
    cross_w,
    up_w,
    down_w,
    norm_gain,
    norm_bias,
    cross_gain,
    cross_bias,
):
    section = lax.axis_index("section")
    is_dec = section == 1
    d = lax.axis_index("dp")
    t = lax.axis_index("tensor")
    core = d % 2
    me = d % 4
    feat = inputs.shape[3]
    chunk = inputs.shape[2]
    half = 2 * chunk
    row_len = 2 * half
    quarter = qkv_w.shape[3]
    n_t = 4

    got = [deal(lax.dynamic_index_in_dim(inputs[0], (t + k) % 2, 0, False), k) for k in range(2)]
    mate = [swap_dp(g, 1) for g in got]

    stack = jnp.concatenate([qkv_w[0], out_w[0].T[None]], axis=0)
    attn_ws = gather_pieces(lax.dynamic_index_in_dim(stack, me, 0, False))
    unit_quarter = up_w.shape[2] // 4
    up_piece = lax.dynamic_slice_in_dim(up_w[0], me * unit_quarter, unit_quarter, 1).T
    down_piece = lax.dynamic_slice_in_dim(down_w[0], me * unit_quarter, unit_quarter, 0)
    up_ws = gather_pieces(up_piece)
    down_ws = gather_pieces(down_piece)
    from_enc = to_decoder(jnp.where(me == 1, cross_w[0, 0], cross_w[0, 1]))
    cross_piece = jnp.where(me == 0, cross_w[0, 0], jnp.where(me == 3, cross_w[0, 1], from_enc))
    cross_ws = gather_pieces(cross_piece)

    own_info = jnp.concatenate(
        [lengths[0], lengths[1], row_flags[:, None], jnp.zeros((2, 7), jnp.int32)], axis=1
    ).astype(F32)
    mate_info = swap_dp(own_info, 1)
    row_info = jnp.where(t // 2 == core, own_info, mate_info)
    row_info = lax.dynamic_index_in_dim(row_info, t % 2, 0, False).astype(jnp.int32)
    flip = core * half + (t % 2) * chunk

    def info_of(lens, causal):
        tail = jnp.stack([row_info[16], flip, causal, me, is_dec.astype(jnp.int32), 0, 0, 0]).astype(jnp.int32)
        return jnp.concatenate([lens, tail])

    src_lens = row_info[0:8]
    tgt_lens = row_info[8:16]
    self_info = info_of(jnp.where(is_dec, tgt_lens, src_lens), is_dec.astype(jnp.int32))
    cross_info = info_of(src_lens, jnp.zeros((), jnp.int32))

    gains = jnp.where(is_dec, norm_gain[1], norm_gain[0])
    shifts = jnp.where(is_dec, norm_bias[1], norm_bias[0])
    gain1, gain3 = gains[0:1], gains[1:2]
    shift1, shift3 = shifts[0:1], shifts[1:2]
    cgain, cshift = cross_gain[None], cross_bias[None]

    f_proj = 2 * half * feat * feat
    f_att = 2 * half * row_len * feat
    f_ffn = 2 * half * feat * up_w.shape[2] * n_t

    rows = (half, feat)
    att_outs = [
        (rows, F32), (rows, F32), ((half, 1), F32), (rows, BF), ((row_len, feat), BF), ((row_len, feat), BF),
        (rows, BF), ((HEADS, 1, half), F32),
    ]
    wall = pltpu.VMEM((4, feat, feat), BF)
    bias_n = pltpu.VMEM((half, row_len), F32)
    bias_t = pltpu.VMEM((row_len, half), F32)
    rd_s = pltpu.VMEM((HEADS, 1, half), F32)

    def attention(info, xq, xk, ws, gain, shift):
        return call(
            functools.partial(attention_kernel, (len(xq), len(xk))), att_outs,
            [info, *xq, *xk, *ws, gain, shift], [wall, bias_n], flops=6 * f_proj + 4 * f_att,
        )

    mid, n1, inv1, q1, k1, v1, att1, lse1 = attention(self_info, got, got + mate, attn_ws, gain1, shift1)
    mem, mem_low, n3e, inv3e = call(
        ffn_forward_kernel, [(rows, F32), (rows, BF), (rows, F32), ((half, 1), F32)],
        [mid, *up_ws, *down_ws, gain3, shift3], flops=2 * f_ffn,
    )

    mem_own = to_decoder(mem_low)
    mem_mate = swap_dp(mem_own, 1)

    cot = jnp.concatenate(
        [deal(lax.dynamic_index_in_dim(cotangent[0], (t + k) % 2, 0, False), k) for k in range(2)], axis=0
    )

    h2, n2, inv2, q2, k2, v2, att2, lse2 = attention(cross_info, [mid], [mem_own, mem_mate], cross_ws, cgain, cshift)
    final, n3d, inv3d, dh2 = call(
        ffn_both_kernel, [(rows, BF), (rows, F32), ((half, 1), F32), (rows, F32)],
        [h2, cot, *up_ws, *down_ws, gain3, shift3],
        [pltpu.VMEM((half, up_w.shape[2] * n_t), F32)], flops=4 * f_ffn,
    )
    dh1, dmem_own, dmem_mate, dbr2, dq2, dk2, dv2, dnorm2 = call(
        cross_backward_kernel,
        [(rows, F32), (rows, BF), (rows, BF), (rows, BF), (rows, BF), ((row_len, feat), BF), ((row_len, feat), BF), ((8, feat), F32)],
        [cross_info, dh2, n2, inv2, cgain, q2, k2, v2, att2, lse2, *cross_ws],
        [wall, bias_t, rd_s, pltpu.VMEM(rows, BF)], flops=6 * f_proj + 8 * f_att,
    )
    dmem = (dmem_own.astype(F32) + swap_dp(dmem_mate, 1).astype(F32)).astype(BF)
    dmem_enc = to_encoder(dmem)
    pieces = [((2, n_t, feat, quarter), BF)] * 2
    cross_keep, cross_send = call(
        cross_weights_kernel, pieces, [cross_info, mid, mem_own, mem_mate, att2, dbr2, dq2, dk2, dv2], flops=6 * f_proj,
    )

    ffn_x = jnp.where(is_dec, h2, mid)
    n3 = jnp.where(is_dec, n3d, n3e)
    inv3 = jnp.where(is_dec, inv3d, inv3e)
    dy3 = cot.astype(F32) + dmem_enc.astype(F32)
    ffn_pieces = [((2, n_t, 2, unit_quarter, feat), BF)] * 2
    do1, ffn_keep, ffn_send, dr1, dbr1, dnorm1 = call(
        ffn_backward_kernel,
        [(rows, BF), *ffn_pieces, (rows, F32), (rows, BF), ((8, feat), F32)],
        [self_info, ffn_x, n3, inv3, dy3, gain3, dh1, n1, inv1, gain1, *up_ws, *down_ws, *attn_ws],
        [wall], flops=5 * f_ffn,
    )
    dq1, dkv_own, dkv_mate = call(
        self_backward_kernel, [(rows, BF), ((2, half, feat), BF), ((2, half, feat), BF)],
        [self_info, q1, k1, v1, do1, att1, lse1],
        [bias_t, rd_s, pltpu.VMEM((row_len, feat), BF), pltpu.VMEM((row_len, feat), BF)], flops=8 * f_att,
    )
    dkv_got = swap_dp(dkv_mate, 1)
    dx, self_keep, self_send = call(
        input_backward_kernel, [(rows, BF), *pieces],
        [self_info, *got, dr1, dq1, dkv_own, dkv_got, att1, dbr1, *attn_ws], [wall], flops=7 * f_proj,
    )

    ffn_sum = spread_pieces(reduce_pieces(ffn_keep, ffn_send))
    self_sum = spread_pieces(reduce_pieces(self_keep, self_send))
    cross_sum = reduce_pieces(cross_keep, cross_send)
    cross_sum = jnp.where(is_dec, cross_sum, to_encoder(cross_sum))
    cross_sum = spread_pieces(cross_sum)

    def matrix(stacked, which):
        return lax.dynamic_index_in_dim(stacked, me ^ which, 0, False).astype(F32)

    qkv_grad = jnp.stack([matrix(self_sum, m) for m in range(3)])
    out_grad = matrix(self_sum, 3).T
    cross_grad = jnp.stack([
        matrix(cross_sum, jnp.where(is_dec, 0, 1)), matrix(cross_sum, jnp.where(is_dec, 3, 2))
    ])
    ffn_true = [matrix(ffn_sum, m) for m in range(4)]
    up_grad = jnp.concatenate([f[0].T for f in ffn_true], axis=1)
    down_grad = jnp.concatenate([f[1] for f in ffn_true], axis=0)

    norms = jnp.concatenate([dnorm1[0:4], dnorm2[0:2], jnp.zeros((2, feat), F32)], axis=0)
    bit = 1
    while bit < lax.axis_size("dp"):
        norms = norms + swap_dp(norms, bit)
        bit *= 2
    norms = norms + swap_tensor(norms, 1)
    norms = norms + swap_tensor(norms, 2)
    other = lax.ppermute(norms, "section", [(0, 1), (1, 0)])
    enc = jnp.where(is_dec, other, norms)
    dec = jnp.where(is_dec, norms, other)
    full_gain = jnp.stack([enc[0:2], dec[0:2]])
    full_bias = jnp.stack([enc[2:4], dec[2:4]])

    def rows_back(value):
        back = [deal_back(value[k * chunk : (k + 1) * chunk], k) for k in range(2)]
        even = t % 2 == 0
        return jnp.stack([jnp.where(even, back[0], back[1]), jnp.where(even, back[1], back[0])])

    out_rows = rows_back(jnp.where(is_dec, final, mem_low))
    grad_rows = rows_back(dx).astype(F32)
    return (
        out_rows[None],
        grad_rows[None],
        qkv_grad[None],
        out_grad[None],
        cross_grad[None],
        up_grad[None],
        down_grad[None],
        full_gain,
        full_bias,
        dec[4],
        dec[5],
    )


def solution(mesh):
    return jax.shard_map(
        body,
        mesh=mesh,
        in_specs=(
            P("section", "dp", "tensor", None),
            P("section", "dp", "tensor", None),
            P(None, "dp", None),
            P("dp"),
            P("section", None, None, "tensor"),
            P("section", "tensor", None),
            P("section", None, None, "tensor"),
            P("section", None, "tensor"),
            P("section", "tensor", None),
            P(),
            P(),
            P(),
            P(),
        ),
        out_specs=(
            P("section", "dp", "tensor", None),
            P("section", "dp", "tensor", None),
            P("section", None, None, "tensor"),
            P("section", "tensor", None),
            P("section", None, None, "tensor"),
            P("section", None, "tensor"),
            P("section", "tensor", None),
            P(),
            P(),
            P(),
            P(),
        ),
        check_vma=False,
    )
```

time: 1450 us -> 389 us (0.27)
  waiting for transfers between devices: 899 us -> 144 us
  matrix products: 212 us -> 0 us
  other arithmetic: 135 us -> 19.4 us
  Pallas kernels: 0 us -> 90.7 us
  starting transfers between devices: 19.6 us -> 98.1 us
  local copies, waits for them, and re-layouts: 89.7 us -> 28.9 us
  blocking collectives: 41.1 us -> 0 us
  loops' own time: 17.7 us -> 0 us
  between operations: 19.2 us -> 1.94 us
    all_gather x18 -> x0, waiting for transfers between devices: 453 us -> none  [the longest x9 211 us: spread_grad(): return lax.all_gather(rows_low, 'tensor', axis=1, tiled=True)]
    reduce_scatter x18 -> x0, waiting for transfers between devices: 385 us -> none  [the longest x9 202 us: collect(): lax.psum_scatter(partial_value.astype(jnp.bfloat16), 'tensor', scatter_di...]
    dot_general x140 -> x0, matrix products: 205 us -> none  [the longest x24 29.6 us: one_block(): jnp.einsum('bqhd,bkhd->bhqk', q_block, k_heads, preferred_element_type=jn...]
    pallas_call x0 -> x9, Pallas kernels: none -> 90.7 us  [call(): pl.pallas_call(kernel, out_shape=tuple((jax.ShapeDtypeStruct(shape, dt) f...]
    ppermute x6 -> x68, waiting for transfers between devices: 56.4 us -> 144 us  [the longest x32 58.1 us: swap_dp(): return lax.ppermute(x, 'dp', [(i, i ^ bit) for i in range(n)])]
    ppermute x6 -> x68, starting transfers between devices: 16.2 us -> 98.1 us  [the longest x32 30.8 us: swap_dp(): return lax.ppermute(x, 'dp', [(i, i ^ bit) for i in range(n)])]
    reduce_sum x36 -> x0, other arithmetic: 47.3 us -> none  [the longest x8 19.5 us: norm_back(): jnp.sum(grad_out * normed, axis=(0, 1))]
    convert_element_type x41 -> x14, other arithmetic: 48.8 us -> 3.66 us  [the longest x3 1.24 us: reduce_pieces(): halves = (keep.astype(F32) + swap_dp(send, 1).astype(F32)).astype(BF)]
  transfers between devices with their start and end apart: 43 -> 68, of which waited for: 40 -> 27; matrix products, arithmetic and copies ran while one was open for 11% -> 7% of each run, Pallas kernels for 0% -> 13%
where the time goes in v1:
time: 389 us; the launch traced here: 383 us
  waiting for transfers between devices  144 us (37%)
  starting transfers between devices  98.1 us (25%)
  Pallas kernels  90.7 us (23%)
  local copies, waits for them, and re-layouts  28.9 us (7%)
  other arithmetic  19.4 us (5%)
    pallas_call x9, Pallas kernels, call(): pl.pallas_call(kernel, out_shape=tuple((jax.ShapeDtypeStruct(shape, dt) f...  90.7 us
    ppermute x32, waiting for transfers between devices, swap_dp(): return lax.ppermute(x, 'dp', [(i, i ^ bit) for i in range(n)])  58.1 us
    ppermute x21, waiting for transfers between devices, shift_tensor(): return lax.ppermute(x, 'tensor', [(i, (i + step) % n) for i in range(n)])  36.2 us
    ppermute x32, starting transfers between devices, swap_dp(): return lax.ppermute(x, 'dp', [(i, i ^ bit) for i in range(n)])  30.8 us
    ppermute x21, starting transfers between devices, shift_tensor(): return lax.ppermute(x, 'tensor', [(i, (i + step) % n) for i in range(n)])  26.9 us
    unnamed x100, local copies, waits for them, and re-layouts  21.2 us
    ppermute x4, starting transfers between devices, deal(): return lax.ppermute(x, ('dp', 'tensor'), deal_route(k))  19.2 us
    ppermute x2, waiting for transfers between devices, to_encoder(): return lax.ppermute(x, 'section', [(1, 0)])  17 us
  transfers between devices with their start and end apart: 68, of which 27 were waited for; matrix products, arithmetic and copies ran while one was open for 7% of the time, Pallas kernels for 13%

profile of v1, /device:TPU:9, one launch (start us, length us, event | category | flops | bytes accessed | tf_op | source)
XLA Modules:
  0.0 383.3 jit_solution(14193736141862631381)
XLA Ops:
  17.4 3.9 %collective-permute-done.5 = bf16[512,128]{1,0:T(8,128)(2,1)S(1)} collective-permute-done((bf16[512,128]{1,0:T(8,128)(2,1)S(1)}, bf16[512,128]{1,0:T(8,128)(2,1)S(1)}, u32[]{:S(2)}, u32[]{:S(2)}) %collective-permute-start.5) | collective-permute-done | bytes 131104 | tf_op jit(solution)/shard_map/ppermute | solution.py:30
  21.3 3.1 collective-permute-start.25
  24.8 3.8 collective-permute-start.1
  30.6 4.6 %collective-permute-start.17 = (bf16[128,512]{1,0:T(8,128)(2,1)S(1)}, bf16[128,512]{1,0:T(8,128)(2,1)S(1)}, u32[]{:S(2)}, u32[]{:S(2)}) collective-permute-start(bf16[128,512]{1,0:T(8,128)(2,1)S(1)} %fusion.24), channel_id=1, source_target_pairs={{0,1},{1,2},{2,3},{3,0},{4,5},{5,6},{6,7},{7,4},{8,9},{9,10},{10,1... | collective-permute-start | bytes 393224 | tf_op jit(solution)/shard_map/ppermute | solution.py:30
  37.2 5.4 %collective-permute-done.18 = bf16[128,512]{1,0:T(8,128)(2,1)S(1)} collective-permute-done((bf16[128,512]{1,0:T(8,128)(2,1)S(1)}, bf16[128,512]{1,0:T(8,128)(2,1)S(1)}, u32[]{:S(2)}, u32[]{:S(2)}) %collective-permute-start.18) | collective-permute-done | bytes 131104 | tf_op jit(solution)/shard_map/ppermute | solution.py:30
  49.1 9.8 %collective-permute-done.2.refs_1_.refs_3_.x1 = bf16[256,512]{1,0:T(8,128)(2,1)S(1)} collective-permute-done((bf16[256,512]{1,0:T(8,128)(2,1)S(1)}, bf16[256,512]{1,0:T(8,128)(2,1)S(1)}, u32[]{:S(2)}, u32[]{:S(2)}) %collective-permute-start.2) | collective-permute-done | bytes 262176 | tf_op jit(solution)/shard_map/ppermute | solution.py:58
  67.0 7.7 %collective-permute-done.15.refs_2_ = bf16[4,128,512]{2,1,0:T(8,128)(2,1)} collective-permute-done((bf16[4,128,512]{2,1,0:T(8,128)(2,1)S(1)}, bf16[4,128,512]{2,1,0:T(8,128)(2,1)}, u32[]{:S(2)}, u32[]{:S(2)}) %collective-permute-start.15) | collective-permute-done | bytes 524320 | tf_op jit(solution)/shard_map/ppermute | solution.py:25
  75.9 10.1 %collective-permute-done.21.refs_6_ = bf16[4,128,512]{2,1,0:T(8,128)(2,1)} collective-permute-done((bf16[4,128,512]{2,1,0:T(8,128)(2,1)S(1)}, bf16[4,128,512]{2,1,0:T(8,128)(2,1)}, u32[]{:S(2)}, u32[]{:S(2)}) %collective-permute-start.21) | collective-permute-done | bytes 524320 | tf_op jit(solution)/shard_map/ppermute | solution.py:25
  96.7 12.2 %shard_map.212 = (f32[512,512]{1,0:T(8,128)S(1)}, f32[512,512]{1,0:T(8,128)S(1)}, f32[512,1]{1,0:T(8,128)S(1)}, bf16[512,512]{1,0:T(8,128)(2,1)S(1)}, bf16[1024,...) custom-call(s32[16]{0:T(128)S(1)} %concatenate.33.info, ...), custom_call_target="tpu_custom_call" | custom-call | flops 3758096384 | bytes 8935488 | tf_op jit(solution)/shard_map/pallas_call | solution.py:429
  113.9 5.8 %shard_map.213 = (f32[512,512]{1,0:T(8,128)}, bf16[512,512]{1,0:T(8,128)(2,1)S(1)}, f32[512,512]{1,0:T(8,128)S(1)}, f32[512,1]{1,0:T(8,128)S(1)}) custom-call(f32[512,512]{1,0:T(8,128)S(1)} %get-tuple-element.56.x_ref.refs_0_.h_ref, bf16[4,128,512]{2,1,0:T(8,128)(2,1)S(1)} %pad_maximum_fusion.2.refs_0_, ...), custom_call_target="tpu_custom_call" | custom-call | flops 2147483648 | bytes 7870464 | tf_op jit(solution)/shard_map/pallas_call | solution.py:429
  120.5 3.4 collective-permute-start.23
  124.5 9.6 %collective-permute-done.23.refs_1_.mem_own = bf16[512,512]{1,0:T(8,128)(2,1)} collective-permute-done((bf16[512,512]{1,0:T(8,128)(2,1)S(1)}, bf16[512,512]{1,0:T(8,128)(2,1)}, u32[]{:S(2)}, u32[]{:S(2)}) %collective-permute-start.23) | collective-permute-done | bytes 524320 | tf_op jit(solution)/shard_map/ppermute | solution.py:39
  136.1 13.6 %collective-permute-start.32 = (bf16[256,512]{1,0:T(8,128)(2,1)}, bf16[256,512]{1,0:T(8,128)(2,1)}, u32[]{:S(2)}, u32[]{:S(2)}) collective-permute-start(bf16[256,512]{1,0:T(8,128)(2,1)} %get-tuple-element.150), channel_id=1, source_target_pairs={{0,0},{1,1},{2,4},{3,5},{4,2},{5,3},{6,6},{7,7},{8,8},{9,9},{10,12... | collective-permute-start | bytes 786440 | tf_op jit(solution)/shard_map/ppermute | solution.py:58
  153.3 5.4 %collective-permute-done.33 = bf16[256,512]{1,0:T(8,128)(2,1)} collective-permute-done((bf16[256,512]{1,0:T(8,128)(2,1)}, bf16[256,512]{1,0:T(8,128)(2,1)}, u32[]{:S(2)}, u32[]{:S(2)}) %collective-permute-start.33) | collective-permute-done | bytes 262176 | tf_op jit(solution)/shard_map/ppermute | solution.py:58
  159.8 13.5 %shard_map.214 = (f32[512,512]{1,0:T(8,128)S(1)}, f32[512,512]{1,0:T(8,128)S(1)}, f32[512,1]{1,0:T(8,128)S(1)}, bf16[512,512]{1,0:T(8,128)(2,1)S(1)}, bf16[1024,...) custom-call(s32[16]{0:T(128)S(1)} %concatenate.32.info, ...), custom_call_target="tpu_custom_call" | custom-call | flops 3758096384 | bytes 9459776 | tf_op jit(solution)/shard_map/pallas_call | solution.py:429
  176.2 8.0 %shard_map.215 = (bf16[512,512]{1,0:T(8,128)(2,1)S(1)}, f32[512,512]{1,0:T(8,128)S(1)}, f32[512,1]{1,0:T(8,128)S(1)}, f32[512,512]{1,0:T(8,128)S(1)}) custom-call(f32[512,512]{1,0:T(8,128)S(1)} %get-tuple-element.58.x_ref, bf16[512,512]{1,0:T(8,128)(2,1)S(1)} %constant_dynamic-update-slice_fusion.cot_ref, ...), custom_call_target="tpu_custom_call" | custom-call | flops 4294967296 | bytes 8394752 | tf_op jit(solution)/shard_map/pallas_call | solution.py:429
  184.3 17.5 %shard_map.216 = (f32[512,512]{1,0:T(8,128)S(1)}, bf16[512,512]{1,0:T(8,128)(2,1)S(1)}, bf16[512,512]{1,0:T(8,128)(2,1)S(1)}, bf16[512,512]{1,0:T(8,128)(2,1)S(1...) custom-call(s32[16]{0:T(128)S(1)} %concatenate.32.info, ...), custom_call_target="tpu_custom_call" | custom-call | flops 5905580032 | bytes 12619840 | tf_op jit(solution)/shard_map/pallas_call | solution.py:429
  202.0 4.4 %collective-permute-start.34 = (bf16[256,512]{1,0:T(8,128)(2,1)S(1)}, bf16[256,512]{1,0:T(8,128)(2,1)S(1)}, u32[]{:S(2)}, u32[]{:S(2)}) collective-permute-start(bf16[256,512]{1,0:T(8,128)(2,1)S(1)} %get-tuple-element.147), channel_id=1, source_target_pairs={{0,0},{1,1},{4,2},{5,3},{2,4},{3,5},{6,6},{7,7},{8,8},{9,9},{12,10... | collective-permute-start | bytes 786440 | tf_op jit(solution)/shard_map/ppermute | solution.py:62
  207.6 3.8 shard_map.220
  214.4 12.8 %collective-permute-done.37 = bf16[512,512]{1,0:T(8,128)(2,1)S(1)} collective-permute-done((bf16[512,512]{1,0:T(8,128)(2,1)S(1)}, bf16[512,512]{1,0:T(8,128)(2,1)S(1)}, u32[]{:S(2)}, u32[]{:S(2)}) %collective-permute-start.37) | collective-permute-done | bytes 524320 | tf_op jit(solution)/shard_map/ppermute | solution.py:43
  228.4 13.6 %shard_map.217 = (bf16[512,512]{1,0:T(8,128)(2,1)S(1)}, bf16[2,4,2,128,512]{4,3,2,1,0:T(8,128)(2,1)}, bf16[2,4,2,128,512]{4,3,2,1,0:T(8,128)(2,1)}, f32[512,512]...) custom-call(s32[16]{0:T(128)S(1)} %concatenate.33.info, ...), custom_call_target="tpu_custom_call" | custom-call | flops 5368709120 | bytes 17850432 | tf_op jit(solution)/shard_map/pallas_call | solution.py:429
  245.3 12.6 %shard_map.218 = (bf16[512,512]{1,0:T(8,128)(2,1)S(1)}, bf16[2,512,512]{2,1,0:T(8,128)(2,1)S(1)}, bf16[2,512,512]{2,1,0:T(8,128)(2,1)S(1)}) custom-call(s32[16]{0:T(128)S(1)} %concatenate.33.info, bf16[512,512]{1,0:T(8,128)(2,1)S(1)} %copy-done.38, bf16[1024,512]{1,0:T(8,128)(2,1)S(1)} %copy-done.34, bf16[1024,512]{1,0:T(8,128)(2,1)S(1)} %copy-done.36, ...), custom_call_target="tpu_custom_call" | custom-call | flops 4294967296 | bytes 6307904 | tf_op jit(solution)/shard_map/pallas_call | solution.py:429
  268.0 6.5 %collective-permute-done.49 = bf16[4,512,128]{2,1,0:T(8,128)(2,1)S(1)} collective-permute-done((bf16[4,512,128]{2,1,0:T(8,128)(2,1)S(1)}, bf16[4,512,128]{2,1,0:T(8,128)(2,1)S(1)}, u32[]{:S(2)}, u32[]{:S(2)}) %collective-permute-start.49) | collective-permute-done | bytes 524320 | tf_op jit(solution)/shard_map/ppermute | solution.py:25
  277.4 3.8 shard_map.219
  281.2 3.3 collective-permute-start.41
  285.3 3.6 collective-permute-done.50
  290.9 4.1 %collective-permute-done.53 = bf16[512,128]{1,0:T(8,128)(2,1)S(1)} collective-permute-done((bf16[512,128]{1,0:T(8,128)(2,1)S(1)}, bf16[512,128]{1,0:T(8,128)(2,1)S(1)}, u32[]{:S(2)}, u32[]{:S(2)}) %collective-permute-start.53) | collective-permute-done | bytes 131104 | tf_op jit(solution)/shard_map/ppermute | solution.py:43
  305.6 10.3 %collective-permute-done.42 = bf16[4,512,128]{2,1,0:T(8,128)(2,1)S(1)} collective-permute-done((bf16[4,512,128]{2,1,0:T(8,128)(2,1)S(1)}, bf16[4,512,128]{2,1,0:T(8,128)(2,1)S(1)}, u32[]{:S(2)}, u32[]{:S(2)}) %collective-permute-start.42) | collective-permute-done | bytes 524320 | tf_op jit(solution)/shard_map/ppermute | solution.py:25
  318.5 19.9 %collective-permute-done.57 = bf16[4,2,128,512]{3,2,1,0:T(8,128)(2,1)S(1)} collective-permute-done((bf16[4,2,128,512]{3,2,1,0:T(8,128)(2,1)S(1)}, bf16[4,2,128,512]{3,2,1,0:T(8,128)(2,1)S(1)}, u32[]{:S(2)}, u32[]{:S(2)}) %collective-permute-start.57) | collective-permute-done | bytes 1048608 | tf_op jit(solution)/shard_map/ppermute | solution.py:25
  342.0 4.9 %collective-permute-start.39 = (bf16[256,512]{1,0:T(8,128)(2,1)S(1)}, bf16[256,512]{1,0:T(8,128)(2,1)S(1)}, u32[]{:S(2)}, u32[]{:S(2)}) collective-permute-start(bf16[256,512]{1,0:T(8,128)(2,1)S(1)} %get-tuple-element.143), channel_id=1, source_target_pairs={{0,0},{1,1},{4,2},{5,3},{2,4},{3,5},{6,6},{7,7},{8,8},{9,9},{12,10... | collective-permute-start | bytes 786440 | tf_op jit(solution)/shard_map/ppermute | solution.py:62
  348.1 18.2 %collective-permute-done.59 = bf16[2,128,512]{2,1,0:T(8,128)(2,1)S(1)} collective-permute-done((bf16[2,128,512]{2,1,0:T(8,128)(2,1)S(1)}, bf16[2,128,512]{2,1,0:T(8,128)(2,1)S(1)}, u32[]{:S(2)}, u32[]{:S(2)}) %collective-permute-start.59) | collective-permute-done | bytes 262176 | tf_op jit(solution)/shard_map/ppermute | solution.py:30
  370.2 4.5 %collective-permute-done.40 = bf16[256,512]{1,0:T(8,128)(2,1)S(1)} collective-permute-done((bf16[256,512]{1,0:T(8,128)(2,1)S(1)}, bf16[256,512]{1,0:T(8,128)(2,1)S(1)}, u32[]{:S(2)}, u32[]{:S(2)}) %collective-permute-start.40) | collective-permute-done | bytes 262176 | tf_op jit(solution)/shard_map/ppermute | solution.py:62
  (306 shorter events, 117.7 us)
Async XLA Ops:
  16.7 18.4 %collective-permute-start.19 = (bf16[128,512]{1,0:T(8,128)(2,1)S(1)}, bf16[128,512]{1,0:T(8,128)(2,1)S(1)}, u32[]{:S(2)}, u32[]{:S(2)}) collective-permute-start(bf16[128,512]{1,0:T(8,128)(2,1)S(1)} %fusion.24), channel_id=1, source_target_pairs={{0,3},{1,0},{2,1},{3,2},{4,7},{5,4},{6,5},{7,6},{8,11},{9,8},{10,9... | collective-permute-start | bytes 393224 | tf_op jit(solution)/shard_map/ppermute | solution.py:30
  24.8 21.0 %collective-permute-start.1 = (bf16[256,512]{1,0:T(8,128)(2,1)S(1)}, bf16[256,512]{1,0:T(8,128)(2,1)S(1)}, u32[]{:S(2)}, u32[]{:S(2)}) collective-permute-start(bf16[256,512]{1,0:T(8,128)(2,1)S(1)} %get-tuple-element.152), channel_id=1, source_target_pairs={{0,0},{1,1},{2,4},{3,5},{4,2},{5,3},{6,6},{7,7},{8,8},{9,9},{10,12... | collective-permute-start | bytes 786440 | tf_op jit(solution)/shard_map/ppermute | solution.py:58
  35.1 23.8 %collective-permute-start.2 = (bf16[256,512]{1,0:T(8,128)(2,1)S(1)}, bf16[256,512]{1,0:T(8,128)(2,1)S(1)}, u32[]{:S(2)}, u32[]{:S(2)}) collective-permute-start(bf16[256,512]{1,0:T(8,128)(2,1)S(1)} %get-tuple-element.151), channel_id=1, source_target_pairs={{0,1},{1,0},{2,5},{3,4},{4,3},{5,2},{6,7},{7,6},{8,9},{9,8},{10,13... | collective-permute-start | bytes 786440 | tf_op jit(solution)/shard_map/ppermute | solution.py:58
  35.1 28.7 %collective-permute-start.9 = (bf16[4,512,128]{2,1,0:T(8,128)(2,1)S(1)}, bf16[4,512,128]{2,1,0:T(8,128)(2,1)S(1)}, u32[]{:S(2)}, u32[]{:S(2)}) collective-permute-start(bf16[4,512,128]{2,1,0:T(8,128)(2,1)S(1)} %pad_maximum_fusion.1.refs_6_.refs_8_.w0), channel_id=1, source_target_pairs={{0,8},{4,12},{8,0},{12,4},{1,9},{5,13},{9,1},{13,5},{2,10},{6,14},... | collective-permute-start | bytes 1572872 | tf_op jit(solution)/shard_map/ppermute | solution.py:25
  42.6 17.4 %collective-permute-start.28 = (bf16[512,128]{1,0:T(8,128)(2,1)S(1)}, bf16[512,128]{1,0:T(8,128)(2,1)}, u32[]{:S(2)}, u32[]{:S(2)}) collective-permute-start(bf16[512,128]{1,0:T(8,128)(2,1)S(1)} %fusion.15), channel_id=1, source_target_pairs={{0,3},{1,0},{2,1},{3,2},{4,7},{5,4},{6,5},{7,6},{8,11},{9,8},{10,9... | collective-permute-start | bytes 393224 | tf_op jit(solution)/shard_map/ppermute | solution.py:30
  45.7 16.3 %collective-permute-start.26 = (bf16[512,128]{1,0:T(8,128)(2,1)S(1)}, bf16[512,128]{1,0:T(8,128)(2,1)S(1)}, u32[]{:S(2)}, u32[]{:S(2)}) collective-permute-start(bf16[512,128]{1,0:T(8,128)(2,1)S(1)} %fusion.15), channel_id=1, source_target_pairs={{0,1},{1,2},{2,3},{3,0},{4,5},{5,6},{6,7},{7,4},{8,9},{9,10},{10,1... | collective-permute-start | bytes 393224 | tf_op jit(solution)/shard_map/ppermute | solution.py:30
  62.0 23.9 %collective-permute-start.21 = (bf16[4,128,512]{2,1,0:T(8,128)(2,1)S(1)}, bf16[4,128,512]{2,1,0:T(8,128)(2,1)}, u32[]{:S(2)}, u32[]{:S(2)}) collective-permute-start(bf16[4,128,512]{2,1,0:T(8,128)(2,1)S(1)} %pad_maximum_fusion.3.refs_4_), channel_id=1, source_target_pairs={{0,8},{4,12},{8,0},{12,4},{1,9},{5,13},{9,1},{13,5},{2,10},{6,14},... | collective-permute-start | bytes 1572872 | tf_op jit(solution)/shard_map/ppermute | solution.py:25
  63.9 26.2 %collective-permute-start.10 = (bf16[4,512,128]{2,1,0:T(8,128)(2,1)S(1)}, bf16[4,512,128]{2,1,0:T(8,128)(2,1)S(1)}, u32[]{:S(2)}, u32[]{:S(2)}) collective-permute-start(bf16[4,512,128]{2,1,0:T(8,128)(2,1)S(1)} %collective-permute-done.9.refs_8_.refs_10_.w2), channel_id=1, source_target_pairs={{0,4},{4,0},{8,12},{12,8},{1,5},{5,1},{9,13},{13,9},{2,6},{6,2},{1... | collective-permute-start | bytes 1572872 | tf_op jit(solution)/shard_map/ppermute | solution.py:25
  65.7 46.8 %collective-permute-start.14 = (bf16[4,128,512]{2,1,0:T(8,128)(2,1)S(1)}, bf16[4,128,512]{2,1,0:T(8,128)(2,1)}, u32[]{:S(2)}, u32[]{:S(2)}) collective-permute-start(bf16[4,128,512]{2,1,0:T(8,128)(2,1)S(1)} %pad_maximum_fusion.2.refs_0_), channel_id=1, source_target_pairs={{0,4},{4,0},{8,12},{12,8},{1,5},{5,1},{9,13},{13,9},{2,6},{6,2},{1... | collective-permute-start | bytes 1572872 | tf_op jit(solution)/shard_map/ppermute | solution.py:25
  66.9 45.6 %collective-permute-start.20 = (bf16[4,128,512]{2,1,0:T(8,128)(2,1)S(1)}, bf16[4,128,512]{2,1,0:T(8,128)(2,1)}, u32[]{:S(2)}, u32[]{:S(2)}) collective-permute-start(bf16[4,128,512]{2,1,0:T(8,128)(2,1)S(1)} %pad_maximum_fusion.3.refs_4_), channel_id=1, source_target_pairs={{0,4},{4,0},{8,12},{12,8},{1,5},{5,1},{9,13},{13,9},{2,6},{6,2},{1... | collective-permute-start | bytes 1572872 | tf_op jit(solution)/shard_map/ppermute | solution.py:25
  74.7 37.8 %collective-permute-start.16 = (bf16[4,128,512]{2,1,0:T(8,128)(2,1)}, bf16[4,128,512]{2,1,0:T(8,128)(2,1)}, u32[]{:S(2)}, u32[]{:S(2)}) collective-permute-start(bf16[4,128,512]{2,1,0:T(8,128)(2,1)} %collective-permute-done.15.refs_2_), channel_id=1, source_target_pairs={{0,4},{4,0},{8,12},{12,8},{1,5},{5,1},{9,13},{13,9},{2,6},{6,2},{1... | collective-permute-start | bytes 1572872 | tf_op jit(solution)/shard_map/ppermute | solution.py:25
  86.0 26.5 %collective-permute-start.22 = (bf16[4,128,512]{2,1,0:T(8,128)(2,1)}, bf16[4,128,512]{2,1,0:T(8,128)(2,1)}, u32[]{:S(2)}, u32[]{:S(2)}) collective-permute-start(bf16[4,128,512]{2,1,0:T(8,128)(2,1)} %collective-permute-done.21.refs_6_), channel_id=1, source_target_pairs={{0,4},{4,0},{8,12},{12,8},{1,5},{5,1},{9,13},{13,9},{2,6},{6,2},{1... | collective-permute-start | bytes 1572872 | tf_op jit(solution)/shard_map/ppermute | solution.py:25
  90.9 33.6 %collective-permute-start.30 = (bf16[4,512,128]{2,1,0:T(8,128)(2,1)}, bf16[4,512,128]{2,1,0:T(8,128)(2,1)}, u32[]{:S(2)}, u32[]{:S(2)}) collective-permute-start(bf16[4,512,128]{2,1,0:T(8,128)(2,1)} %pad_maximum_fusion.4.refs_3_.w0), channel_id=1, source_target_pairs={{0,8},{4,12},{8,0},{12,4},{1,9},{5,13},{9,1},{13,5},{2,10},{6,14},... | collective-permute-start | bytes 1572872 | tf_op jit(solution)/shard_map/ppermute | solution.py:25
  123.9 35.8 %collective-permute-start.29 = (bf16[4,512,128]{2,1,0:T(8,128)(2,1)}, bf16[4,512,128]{2,1,0:T(8,128)(2,1)}, u32[]{:S(2)}, u32[]{:S(2)}) collective-permute-start(bf16[4,512,128]{2,1,0:T(8,128)(2,1)} %pad_maximum_fusion.4.refs_3_.w0), channel_id=1, source_target_pairs={{0,4},{4,0},{8,12},{12,8},{1,5},{5,1},{9,13},{13,9},{2,6},{6,2},{1... | collective-permute-start | bytes 1572872 | tf_op jit(solution)/shard_map/ppermute | solution.py:25
  124.5 35.2 %collective-permute-start.31 = (bf16[4,512,128]{2,1,0:T(8,128)(2,1)}, bf16[4,512,128]{2,1,0:T(8,128)(2,1)}, u32[]{:S(2)}, u32[]{:S(2)}) collective-permute-start(bf16[4,512,128]{2,1,0:T(8,128)(2,1)} %collective-permute-done.30.refs_5_.w2), channel_id=1, source_target_pairs={{0,4},{4,0},{8,12},{12,8},{1,5},{5,1},{9,13},{13,9},{2,6},{6,2},{1... | collective-permute-start | bytes 1572872 | tf_op jit(solution)/shard_map/ppermute | solution.py:25
  134.1 25.6 %collective-permute-start.24 = (bf16[512,512]{1,0:T(8,128)(2,1)}, bf16[512,512]{1,0:T(8,128)(2,1)}, u32[]{:S(2)}, u32[]{:S(2)}) collective-permute-start(bf16[512,512]{1,0:T(8,128)(2,1)} %collective-permute-done.23.refs_1_.mem_own), channel_id=1, source_target_pairs={{0,4},{4,0},{8,12},{12,8},{1,5},{5,1},{9,13},{13,9},{2,6},{6,2},{1... | collective-permute-start | bytes 1572872 | tf_op jit(solution)/shard_map/ppermute | solution.py:25
  136.1 16.3 %collective-permute-start.32 = (bf16[256,512]{1,0:T(8,128)(2,1)}, bf16[256,512]{1,0:T(8,128)(2,1)}, u32[]{:S(2)}, u32[]{:S(2)}) collective-permute-start(bf16[256,512]{1,0:T(8,128)(2,1)} %get-tuple-element.150), channel_id=1, source_target_pairs={{0,0},{1,1},{2,4},{3,5},{4,2},{5,3},{6,6},{7,7},{8,8},{9,9},{10,12... | collective-permute-start | bytes 786440 | tf_op jit(solution)/shard_map/ppermute | solution.py:58
  202.0 41.3 %collective-permute-start.34 = (bf16[256,512]{1,0:T(8,128)(2,1)S(1)}, bf16[256,512]{1,0:T(8,128)(2,1)S(1)}, u32[]{:S(2)}, u32[]{:S(2)}) collective-permute-start(bf16[256,512]{1,0:T(8,128)(2,1)S(1)} %get-tuple-element.147), channel_id=1, source_target_pairs={{0,0},{1,1},{4,2},{5,3},{2,4},{3,5},{6,6},{7,7},{8,8},{9,9},{12,10... | collective-permute-start | bytes 786440 | tf_op jit(solution)/shard_map/ppermute | solution.py:62
  206.3 36.9 %collective-permute-start.35 = (bf16[256,512]{1,0:T(8,128)(2,1)S(1)}, bf16[256,512]{1,0:T(8,128)(2,1)S(1)}, u32[]{:S(2)}, u32[]{:S(2)}) collective-permute-start(bf16[256,512]{1,0:T(8,128)(2,1)S(1)} %get-tuple-element.148), channel_id=1, source_target_pairs={{1,0},{0,1},{5,2},{4,3},{3,4},{2,5},{7,6},{6,7},{9,8},{8,9},{13,10... | collective-permute-start | bytes 786440 | tf_op jit(solution)/shard_map/ppermute | solution.py:62
  211.4 47.4 %collective-permute-start.48 = (bf16[2,4,512,128]{3,2,1,0:T(8,128)(2,1)S(1)}, bf16[2,4,512,128]{3,2,1,0:T(8,128)(2,1)S(1)}, u32[]{:S(2)}, u32[]{:S(2)}) collective-permute-start(bf16[2,4,512,128]{3,2,1,0:T(8,128)(2,1)S(1)} %get-tuple-element.96), channel_id=1, source_target_pairs={{0,4},{4,0},{8,12},{12,8},{1,5},{5,1},{9,13},{13,9},{2,6},{6,2},{1... | collective-permute-start | bytes 3145736 | tf_op jit(solution)/shard_map/ppermute | solution.py:25
  257.9 19.5 %collective-permute-start.38 = (bf16[2,512,512]{2,1,0:T(8,128)(2,1)S(1)}, bf16[2,512,512]{2,1,0:T(8,128)(2,1)S(1)}, u32[]{:S(2)}, u32[]{:S(2)}) collective-permute-start(bf16[2,512,512]{2,1,0:T(8,128)(2,1)S(1)} %get-tuple-element.86), channel_id=1, source_target_pairs={{0,4},{4,0},{8,12},{12,8},{1,5},{5,1},{9,13},{13,9},{2,6},{6,2},{1... | collective-permute-start | bytes 3145736 | tf_op jit(solution)/shard_map/ppermute | solution.py:25
  265.6 37.7 %collective-permute-start.56 = (bf16[2,4,2,128,512]{4,3,2,1,0:T(8,128)(2,1)}, bf16[2,4,2,128,512]{4,3,2,1,0:T(8,128)(2,1)S(1)}, u32[]{:S(2)}, u32[]{:S(2)}) collective-permute-start(bf16[2,4,2,128,512]{4,3,2,1,0:T(8,128)(2,1)} %get-tuple-element.98), channel_id=1, source_target_pairs={{0,4},{4,0},{8,12},{12,8},{1,5},{5,1},{9,13},{13,9},{2,6},{6,2},{1... | collective-permute-start | bytes 6291464 | tf_op jit(solution)/shard_map/ppermute | solution.py:25
  281.2 20.8 %collective-permute-start.41 = (bf16[2,4,512,128]{3,2,1,0:T(8,128)(2,1)S(1)}, bf16[2,4,512,128]{3,2,1,0:T(8,128)(2,1)S(1)}, u32[]{:S(2)}, u32[]{:S(2)}) collective-permute-start(bf16[2,4,512,128]{3,2,1,0:T(8,128)(2,1)S(1)} %get-tuple-element.90), channel_id=1, source_target_pairs={{0,4},{4,0},{8,12},{12,8},{1,5},{5,1},{9,13},{13,9},{2,6},{6,2},{1... | collective-permute-start | bytes 3145736 | tf_op jit(solution)/shard_map/ppermute | solution.py:25
  304.4 34.0 %collective-permute-start.57 = (bf16[4,2,128,512]{3,2,1,0:T(8,128)(2,1)S(1)}, bf16[4,2,128,512]{3,2,1,0:T(8,128)(2,1)S(1)}, u32[]{:S(2)}, u32[]{:S(2)}) collective-permute-start(bf16[4,2,128,512]{3,2,1,0:T(8,128)(2,1)S(1)} %slice_bitcast_fusion), channel_id=1, source_target_pairs={{0,8},{4,12},{8,0},{12,4},{1,9},{5,13},{9,1},{13,5},{2,10},{6,14},... | collective-permute-start | bytes 3145736 | tf_op jit(solution)/shard_map/ppermute | solution.py:25
  316.1 23.7 %collective-permute-start.45 = (bf16[512,128]{1,0:T(8,128)(2,1)S(1)}, bf16[512,128]{1,0:T(8,128)(2,1)S(1)}, u32[]{:S(2)}, u32[]{:S(2)}) collective-permute-start(bf16[512,128]{1,0:T(8,128)(2,1)S(1)} %get-tuple-element.139), channel_id=1, source_target_pairs={{0,1},{1,2},{2,3},{3,0},{4,5},{5,6},{6,7},{7,4},{8,9},{9,10},{10,1... | collective-permute-start | bytes 393224 | tf_op jit(solution)/shard_map/ppermute | solution.py:30
  316.1 25.9 %collective-permute-start.44 = (bf16[512,128]{1,0:T(8,128)(2,1)S(1)}, bf16[512,128]{1,0:T(8,128)(2,1)S(1)}, u32[]{:S(2)}, u32[]{:S(2)}) collective-permute-start(bf16[512,128]{1,0:T(8,128)(2,1)S(1)} %get-tuple-element.140), channel_id=1, source_target_pairs={{0,2},{1,3},{2,0},{3,1},{4,6},{5,7},{6,4},{7,5},{8,10},{9,11},{10,... | collective-permute-start | bytes 393224 | tf_op jit(solution)/shard_map/ppermute | solution.py:30
  317.1 29.8 %collective-permute-start.43 = (bf16[512,128]{1,0:T(8,128)(2,1)S(1)}, bf16[512,128]{1,0:T(8,128)(2,1)S(1)}, u32[]{:S(2)}, u32[]{:S(2)}) collective-permute-start(bf16[512,128]{1,0:T(8,128)(2,1)S(1)} %get-tuple-element.138), channel_id=1, source_target_pairs={{0,3},{1,0},{2,1},{3,2},{4,7},{5,4},{6,5},{7,6},{8,11},{9,8},{10,9... | collective-permute-start | bytes 393224 | tf_op jit(solution)/shard_map/ppermute | solution.py:30
  338.8 27.4 %collective-permute-start.59 = (bf16[2,128,512]{2,1,0:T(8,128)(2,1)S(1)}, bf16[2,128,512]{2,1,0:T(8,128)(2,1)S(1)}, u32[]{:S(2)}, u32[]{:S(2)}) collective-permute-start(bf16[2,128,512]{2,1,0:T(8,128)(2,1)S(1)} %get-tuple-element.118), channel_id=1, source_target_pairs={{0,2},{1,3},{2,0},{3,1},{4,6},{5,7},{6,4},{7,5},{8,10},{9,11},{10,... | collective-permute-start | bytes 786440 | tf_op jit(solution)/shard_map/ppermute | solution.py:30
  339.8 29.2 %collective-permute-start.58 = (bf16[2,128,512]{2,1,0:T(8,128)(2,1)S(1)}, bf16[2,128,512]{2,1,0:T(8,128)(2,1)S(1)}, u32[]{:S(2)}, u32[]{:S(2)}) collective-permute-start(bf16[2,128,512]{2,1,0:T(8,128)(2,1)S(1)} %get-tuple-element.116), channel_id=1, source_target_pairs={{0,3},{1,0},{2,1},{3,2},{4,7},{5,4},{6,5},{7,6},{8,11},{9,8},{10,9... | collective-permute-start | bytes 786440 | tf_op jit(solution)/shard_map/ppermute | solution.py:30
  342.0 28.2 %collective-permute-start.39 = (bf16[256,512]{1,0:T(8,128)(2,1)S(1)}, bf16[256,512]{1,0:T(8,128)(2,1)S(1)}, u32[]{:S(2)}, u32[]{:S(2)}) collective-permute-start(bf16[256,512]{1,0:T(8,128)(2,1)S(1)} %get-tuple-element.143), channel_id=1, source_target_pairs={{0,0},{1,1},{4,2},{5,3},{2,4},{3,5},{6,6},{7,7},{8,8},{9,9},{12,10... | collective-permute-start | bytes 786440 | tf_op jit(solution)/shard_map/ppermute | solution.py:62
  346.9 27.8 %collective-permute-start.40 = (bf16[256,512]{1,0:T(8,128)(2,1)S(1)}, bf16[256,512]{1,0:T(8,128)(2,1)S(1)}, u32[]{:S(2)}, u32[]{:S(2)}) collective-permute-start(bf16[256,512]{1,0:T(8,128)(2,1)S(1)} %get-tuple-element.144), channel_id=1, source_target_pairs={{1,0},{0,1},{5,2},{4,3},{3,4},{2,5},{7,6},{6,7},{9,8},{8,9},{13,10... | collective-permute-start | bytes 786440 | tf_op jit(solution)/shard_map/ppermute | solution.py:62
  347.1 27.7 %collective-permute-start.46 = (bf16[512,128]{1,0:T(8,128)(2,1)S(1)}, bf16[512,128]{1,0:T(8,128)(2,1)S(1)}, u32[]{:S(2)}, u32[]{:S(2)}) collective-permute-start(bf16[512,128]{1,0:T(8,128)(2,1)S(1)} %fusion.13), channel_id=1, source_target_pairs={{0,8},{4,12},{8,0},{12,4},{1,9},{5,13},{9,1},{13,5},{2,10},{6,14},... | collective-permute-start | bytes 393224 | tf_op jit(solution)/shard_map/ppermute | solution.py:25
  (84 other events, 957.9 us)
